TPU v7x, 32 devices: a whole 2x2x4 slice. The times are simulated.
32 devices in a mesh: grp: 2 (over core), dp: 16 (over z, y, x).
Axes of the slice: x: 2, y: 2, z: 4, core: 2. Of those that a mesh axis runs over, the one named last changes fastest.
Arguments:
- tokens: bfloat16 [4096, 2048], P(('grp', 'dp')), may hold values from -6 to 6
- segments: int32 [4096], P('grp'), may hold values from 0 to 66, as said below
- routes: int32 [4096, 8], P(('grp', 'dp')), may hold values from 0 to 15, all different within a row; in each aligned block of 128 rows (0 to 127, 128 to 255, ...) at most 80 rows name the same one
- route_weight: float32 [4096, 8], P(('grp', 'dp')), may hold values from 0.06 to 0.19
- capacity: int32 [1], replicated, may hold values from 768 to 1279
- norm_gain: float32 [2, 2048], replicated, may hold values from 0.5 to 1.5
- qkv_weight: bfloat16 [6144, 2048], P('dp'), may hold values from -0.125 to 0.125
- out_weight: bfloat16 [2048, 2048], P('dp'), may hold values from -1 to 1
- gate_weight: bfloat16 [16, 2048, 1024], P('dp'), may hold values from -0.125 to 0.125
- up_weight: bfloat16 [16, 2048, 1024], P('dp'), may hold values from -0.125 to 0.125
- down_weight: bfloat16 [16, 1024, 2048], P('dp'), may hold values from -0.75 to 0.75
- cotangent: bfloat16 [4096, 2048], P(('grp', 'dp')), may hold values from -6 to 6
Outputs:
- layer_out: bfloat16 [4096, 2048], P(('grp', 'dp'))
- tokens_grad: float32 [4096, 2048], P(('grp', 'dp'))
- qkv_weight_grad: float32 [6144, 2048], P('dp')
- out_weight_grad: float32 [2048, 2048], P('dp')
- gate_weight_grad: float32 [16, 2048, 1024], P('dp')
- up_weight_grad: float32 [16, 2048, 1024], P('dp')
- down_weight_grad: float32 [16, 1024, 2048], P('dp')
- norm_gain_grad: float32 [2, 2048], replicated
- stats: float32 [2, 3], P('grp')
Inputs may be any that keep to these rules, and one draw needn't show every extreme that they name: `segments`: in each sequence of 2048 tokens, numbers never fall except to 0, which marks the padding that ends the sequence; one document covers all but at most 64 tokens at each end. `routes`: A token names 8 different experts; among the 128 tokens of one device no expert is named more than 80 times.
All inputs are finite; a program needn't handle non-finite values.
Results may differ from a plain program's by a relative error of at most 0.023.
Values may be sent and summed in bfloat16 or wider, within the bound.
A program may use at most 384 MiB of HBM per device.

v0:
```python
import functools

import jax
import jax.numpy as jnp
import numpy as np
from jax import lax
from jax.experimental import pallas as pl
from jax.experimental.pallas import tpu as pltpu
from jax.sharding import PartitionSpec as P

H = 16
HD = 128
TOPK = 8
EPS = 1e-06
THETA = 50000.0
MESH = pl.DeviceIdType.MESH
MIB = 2**20
BF = jnp.bfloat16
F32 = jnp.float32
SCALE = HD**-0.5
LOG2E = 1.4426950408889634


def places():
    me = lax.axis_index("dp")
    z, y, x = me // 4, (me // 2) % 2, me % 2
    xor = [z, z + 1 - 2 * (z % 2), (z + 2) % 4, 3 - z]
    at = lambda k, yy, xx: xor[k] * 4 + yy * 2 + xx
    return dict(
        me=me,
        col=[at(k, y, x) for k in range(4)],
        X=[at(k, y, 1 - x) for k in range(4)],
        Y=[at(k, 1 - y, x) for k in range(4)],
        D=[at(k, 1 - y, 1 - x) for k in range(4)],
    )


def barrier(targets, pair=False):
    sem = pltpu.get_barrier_semaphore()
    for t in targets:
        pl.semaphore_signal(sem, inc=1, device_id={"dp": t}, device_id_type=MESH)
    count = len(targets)
    if pair:
        pl.semaphore_signal(sem, inc=1, device_id={"grp": partner()}, device_id_type=MESH)
        count += 1
    pl.semaphore_wait(sem, count)


def partner():
    g = lax.axis_index("grp")
    return g + 1 - 2 * (g % 2)


def push(src, dst, send, recv, to):
    c = pltpu.make_async_remote_copy(
        src_ref=src, dst_ref=dst, send_sem=send, recv_sem=recv,
        device_id={"dp": to}, device_id_type=MESH,
    )
    c.start()
    return c


def push_pair(src, dst, send, recv):
    c = pltpu.make_async_remote_copy(
        src_ref=src, dst_ref=dst, send_sem=send, recv_sem=recv,
        device_id={"grp": partner()}, device_id_type=MESH,
    )
    c.start()
    return c


GATHER_SEMS = [pltpu.SemaphoreType.DMA((4,))] * 6 + [pltpu.SemaphoreType.DMA((4, 2))] * 2 + [pltpu.SemaphoreType.DMA]


class Gather:
    def __init__(self, src, dst, rows, sems, first=0):
        self.src, self.dst, self.rows, self.sems, self.first, self.p = src, dst, rows, sems, first, places()

    def block(self, b):
        return self.dst.at[b, pl.ds(self.first, self.rows)]

    def part(self, b, h):
        half = self.rows // 2
        return self.dst.at[b, pl.ds(self.first + h * half, half)]

    def begin(self):
        zs, zr, xs, xr, ys, yr, _, _, own = self.sems
        p, src = self.p, self.src
        me = p["me"]
        self.mine = pltpu.make_async_copy(src, self.block(me), own)
        self.mine.start()
        self.xc = {0: push(src, self.block(me), xs.at[0], xr.at[0], p["X"][0])}
        self.yc = {0: push(src, self.block(me), ys.at[0], yr.at[0], p["Y"][0])}
        self.zc = {k: push(src, self.block(me), zs.at[k], zr.at[k], p["col"][k]) for k in (1, 2, 3)}
        self.dc = {}

    def near(self, k):
        _, _, xs, xr, ys, yr, _, _, _ = self.sems
        p = self.p
        self.zc[k].wait_recv()
        b = self.block(p["col"][k])
        self.xc[k] = push(b, b, xs.at[k], xr.at[k], p["X"][0])
        self.yc[k] = push(b, b, ys.at[k], yr.at[k], p["Y"][0])

    def far(self, k):
        ds, dr = self.sems[6:8]
        p = self.p
        b = self.part(p["X"][k], 0)
        self.xc[k].wait_recv()
        self.dc[k, 0] = push(b, b, ds.at[k, 0], dr.at[k, 0], p["Y"][0])
        b = self.part(p["Y"][k], 1)
        self.yc[k].wait_recv()
        self.dc[k, 1] = push(b, b, ds.at[k, 1], dr.at[k, 1], p["X"][0])

    def step(self, k):
        self.far(k)
        if k < 3:
            self.near(k + 1)

    def ready(self, k):
        if k == 0:
            self.mine.wait()
        self.dc[k, 0].wait_recv()
        self.dc[k, 1].wait_recv()

    def end(self):
        for group in (self.xc, self.yc, self.zc, self.dc):
            for c in group.values():
                c.wait_send()

    def all(self):
        for k in range(4):
            self.step(k)
        for k in range(4):
            self.ready(k)
        self.end()


def gather_targets():
    p = places()
    return [p["col"][1], p["col"][2], p["col"][3], p["X"][0], p["Y"][0]]


SCATTER_SEMS = [pltpu.SemaphoreType.DMA((4, 2))] * 2 + [pltpu.SemaphoreType.DMA((4,))] * 6


def scatter_bufs(rows, width):
    return [
        pltpu.VMEM((8, rows // 2, width), BF),
        pltpu.VMEM((4, rows, width), BF),
        pltpu.VMEM((4, rows, width), BF),
        pltpu.VMEM((4, rows, width), BF),
    ]


class Scatter:
    def __init__(self, part, out, rows, bufs, sems):
        self.part, self.out, self.half, self.bufs, self.sems, self.p = part, out, rows // 2, bufs, sems, places()
        self.da, self.db, self.xc, self.yc, self.zc = {}, {}, {}, {}, {}

    def far(self, k):
        ds, dr = self.sems[:2]
        rd, h, p = self.bufs[0], self.half, self.p
        b = p["D"][k]
        self.da[k] = push(self.part.at[b, pl.ds(0, h)], rd.at[2 * k], ds.at[k, 0], dr.at[k, 0], p["Y"][0])
        self.db[k] = push(self.part.at[b, pl.ds(h, h)], rd.at[2 * k + 1], ds.at[k, 1], dr.at[k, 1], p["X"][0])

    def near(self, k):
        _, _, xs, xr, ys, yr, _, _ = self.sems
        rd, rx, ry, _ = self.bufs
        part, h, p = self.part, self.half, self.p
        b = p["X"][k]
        if k in self.da:
            self.da[k].wait_recv()
        part[b, pl.ds(0, h)] = (part[b, pl.ds(0, h)].astype(F32) + rd[2 * k].astype(F32)).astype(BF)
        self.xc[k] = push(part.at[b], rx.at[k], xs.at[k], xr.at[k], p["X"][0])
        b = p["Y"][k]
        if k in self.db:
            self.db[k].wait_recv()
        part[b, pl.ds(h, h)] = (part[b, pl.ds(h, h)].astype(F32) + rd[2 * k + 1].astype(F32)).astype(BF)
        self.yc[k] = push(part.at[b], ry.at[k], ys.at[k], yr.at[k], p["Y"][0])

    def along(self, k):
        zs, zr = self.sems[6:]
        _, rx, ry, rz = self.bufs
        part = self.part
        b = self.p["col"][k]
        self.xc[k].wait_recv()
        self.yc[k].wait_recv()
        total = part[b].astype(F32) + rx[k].astype(F32) + ry[k].astype(F32)
        if k:
            part[b] = total.astype(BF)
            self.zc[k] = push(part.at[b], rz.at[k], zs.at[k], zr.at[k], b)
        else:
            self.out[...] = total

    def end(self):
        for k in (1, 2, 3):
            self.zc[k].wait_recv()
            self.out[...] += self.bufs[3][k].astype(F32)
        for group in (self.da, self.db, self.xc, self.yc, self.zc):
            for c in group.values():
                c.wait_send()

    def all(self):
        order = (1, 2, 3, 0)
        for k in order:
            self.far(k)
        for k in order:
            self.near(k)
        for k in order:
            self.along(k)
        self.end()


ANY = pl.BlockSpec(memory_space=pl.ANY)
VM = pl.BlockSpec(memory_space=pltpu.VMEM)


def params(cid, vmem=60):
    return pltpu.CompilerParams(collective_id=cid, has_side_effects=True, vmem_limit_bytes=vmem * MIB)


def rmsnorm(field, gain_row):
    return field * lax.rsqrt(jnp.mean(field * field, -1, keepdims=True) + EPS) * gain_row


def rmsnorm_pull(field, gain_row, grad):
    r = lax.rsqrt(jnp.mean(field * field, -1, keepdims=True) + EPS)
    scaled = grad * gain_row
    back = r * scaled - field * (r * r * r * jnp.mean(scaled * field, -1, keepdims=True))
    return back, grad * field * r


def column(rows, b):
    return jnp.broadcast_to(rows[pl.ds(b, 1), :], (8, rows.shape[1])).T[:, :1]


def dot(a, b, ca, cb):
    return lax.dot_general(a, b, (((ca,), (cb,)), ((), ())), preferred_element_type=F32)


def front_kernel(
    tok, gain, m_ref, w_ref, o_ref, cosf, sinf, seg, sk,
    nall_o, mall, wh_o, q, k, v, lse, ctx, oall,
    n_ref, nall, wh, ctxh, ms, mr, mo, ws, wr, ps, pr, wo, no, cs, cr, co, os_, or_, *sems,
):
    me = lax.axis_index("dp")
    core = lax.axis_index("grp") % 2
    hr = HD // 2
    blk = lambda b: pl.ds(pl.multiple_of(b * HD, HD), HD)
    half = lambda s, c: pl.ds(pl.multiple_of(s * HD + c * hr, hr), hr)
    n_ref[...] = rmsnorm(tok[...].astype(F32), gain[...]).astype(BF)
    barrier([lax.rem(me + d, 16) for d in range(1, 16)], pair=True)
    g = Gather(n_ref, nall, n_ref.shape[0], sems[:9])
    go = Gather(o_ref.at[half(0, core)], oall, hr, sems[9:], pl.multiple_of(core * hr, hr))
    g.begin()
    own = pltpu.make_async_copy(m_ref, mall.at[me], mo)
    own.start()
    mc = [push(m_ref, mall.at[me], ms.at[d], mr.at[d], lax.rem(me + d, 16)) for d in range(1, 16)]
    for l in range(3):
        b = 3 * me + l
        to, slot = lax.rem(b, 16), b // 16
        src, dst = w_ref.at[half(l, core)], wh.at[half(slot, core)]

        @pl.when(to != me)
        def _():
            push(src, dst, ws.at[l], wr.at[slot], to)

        @pl.when(to == me)
        def _():
            pltpu.make_async_copy(src, dst, wr.at[slot]).start()

    def project(b, carry):
        row = blk(b)
        out = dot(nall[b], wh[...], 1, 1)
        turn = lambda a: (a * cosf[row] + pltpu.roll(a, HD // 2, 1) * sinf[row]).astype(BF)
        q[row] = turn(out[:, :HD])
        k[row] = turn(out[:, HD : 2 * HD])
        v[row] = out[:, 2 * HD :].astype(BF)
        return carry

    def project_plane(c):
        lax.fori_loop(0, 4, lambda j, carry: project(place_of(c, j), carry), 0)

    for c in range(4):
        g.step(c)
        if c == WAIT_AT:
            pc = []
            for s in range(3):
                dst = wh.at[half(s, core)]
                pltpu.make_async_copy(dst, dst, wr.at[s]).wait()
                pc.append(push_pair(dst, dst, ps.at[s], pr.at[s]))
        if c == BEGIN_AT:
            go.begin()
        if c == WAIT_AT:
            for p in pc:
                p.wait_recv()
        g.ready(c)
        if c == WAIT_AT:
            for e in range(c):
                project_plane(e)
        if c >= WAIT_AT:
            project_plane(c)
    saves = [pltpu.make_async_copy(nall, nall_o, no), pltpu.make_async_copy(wh, wh_o, wo)]
    for c in saves:
        c.start()

    def hop(d):
        to = lax.rem(me + d, 16)
        return pltpu.make_async_remote_copy(
            src_ref=ctxh.at[blk(to)], dst_ref=ctx.at[:, blk(me)], send_sem=cs.at[d], recv_sem=cr.at[d],
            device_id={"dp": to}, device_id_type=MESH,
        )

    def attend_rows(d, carry):
        b = lax.rem(me + d, 16)
        row = blk(b)
        s = dot(q[row], k[...], 1, 1)
        s = jnp.where(column(seg, b) == sk[...], s, -1e30)
        peak = jnp.maximum(jnp.max(s, -1, keepdims=True), -1e29)
        ex = jnp.exp2((s - peak) * (SCALE * LOG2E))
        total = jnp.maximum(jnp.sum(ex, -1, keepdims=True), 1.0)
        prob = (ex * (1.0 / total)).astype(BF)
        ctxh[row] = jnp.dot(prob, v[...], preferred_element_type=F32).astype(BF)
        lse[row] = peak * (SCALE * LOG2E) + jnp.log2(total)
        return carry

    def attend_send(d, carry):
        attend_rows(d, carry)
        hop(d).start()
        return carry

    lax.fori_loop(1, 8, attend_send, 0)
    go.step(0)
    lax.fori_loop(8, 16, attend_send, 0)
    attend_rows(0, 0)
    stay = pltpu.make_async_copy(ctxh.at[blk(me)], ctx.at[:, blk(me)], co)
    stay.start()
    for c in (1, 2, 3):
        go.step(c)
    for c in range(4):
        go.ready(c)
    here = oall.at[:, pl.ds(pl.multiple_of(core * hr, hr), hr)]
    oc = push_pair(here, here, os_, or_)
    g.end()
    go.end()
    own.wait()
    for c in mc:
        c.wait()
    for l in range(3):
        src = w_ref.at[half(l, core)]

        @pl.when(lax.rem(3 * me + l, 16) != me)
        def _():
            pltpu.make_async_copy(src, src, ws.at[l]).wait()

    for p in pc:
        p.wait_send()
    for c in saves:
        c.wait()
    stay.wait()
    for d in range(1, 16):
        hop(d).wait()
    oc.wait()


def front(tokens, gain, meta, w, wo, cosf, sinf, seg, sk, cid):
    rows, width = tokens.shape
    seq = cosf.shape[0]
    sem = lambda *shape: pltpu.SemaphoreType.DMA(shape) if shape else pltpu.SemaphoreType.DMA
    b = lambda *shape: jax.ShapeDtypeStruct(shape, BF)
    f = lambda *shape: jax.ShapeDtypeStruct(shape, F32)
    v = lambda *shape: pltpu.VMEM(shape, BF)
    return pl.pallas_call(
        front_kernel,
        out_shape=[
            b(16, rows, width), f(16, *meta.shape), b(3 * HD, width),
            b(seq, HD), b(seq, HD), b(seq, HD), f(seq, 1), b(rows, width), b(16, rows, width),
        ],
        in_specs=[VM, VM] + [ANY] * 3 + [VM] * 4,
        out_specs=[ANY] * 3 + [VM] * 4 + [ANY] * 2,
        scratch_shapes=[v(rows, width), v(16, rows, width), v(3 * HD, width), v(seq, HD)]
        + [sem(16), sem(16), sem(), sem(3), sem(3), sem(3), sem(3), sem(), sem()]
        + [sem(16), sem(16), sem(), sem(), sem()]
        + GATHER_SEMS * 2,
        compiler_params=params(cid),
        name="front",
    )(tokens, gain, meta, w, wo, cosf, sinf, seg, sk)


SLOTS = 80
WAIT_AT = 2
BEGIN_AT = 2
COLS = 512


def place_of(k, j):
    me = lax.axis_index("dp")
    z, y, x = me // 4, (me // 2) % 2, me % 2
    zk = [z, z + 1 - 2 * (z % 2), (z + 2) % 4, 3 - z][k]
    jy, jx = j // 2, j % 2
    return zk * 4 + (y + jy - 2 * y * jy) * 2 + (x + jx - 2 * x * jx)


def expert_kernel(
    ctx, wout, tok, gain, cot, meta, cap, wg_h, wu_h, wd_h,
    att, n2g, p1, rdm, xr_o, pg_o, hid_o, gg_o, ug_o,
    n2, rank, coef, pick, sw, nall, call, part, stage, wg, wu, wd, xr, pg, hid, gg, ug, rd, rx, ry, rz,
    wosem, wsem, osem, psem, ms, mr, *sems,
):
    rows, width = ctx.shape
    wload = pltpu.make_async_copy(wout, part, wosem)
    wload.start()
    barrier(gather_targets())
    gn = Gather(n2, nall, rows, sems[:9])
    gc = Gather(cot, call, rows, sems[9:18])
    sc = Scatter(part, n2g, rows, (rd, rx, ry, rz), sems[18:])
    sm = Scatter(p1, None, rows, (rdm, None, None, None), (ms, mr))
    gc.begin()
    loads = [pltpu.make_async_copy(a, b, wsem.at[i]) for i, (a, b) in enumerate([(wg_h, wg), (wu_h, wu), (wd_h, wd)])]
    me = lax.axis_index("dp").astype(F32)
    hits = [meta[:, r, :] == me for r in range(TOPK)]
    member = sum(h.astype(F32) for h in hits)
    coef[...] = sum(jnp.where(h, meta[:, TOPK + r, :], 0.0) for r, h in enumerate(hits))
    i0, i1 = lax.broadcasted_iota(jnp.int32, (HD, HD), 0), lax.broadcasted_iota(jnp.int32, (HD, HD), 1)
    local = dot(member.astype(BF), (i0 < i1).astype(BF), 1, 0)
    count = jnp.broadcast_to(jnp.sum(member, 1, keepdims=True), member.shape).astype(BF)
    j0, j1 = lax.broadcasted_iota(jnp.int32, (16, 16), 0), lax.broadcasted_iota(jnp.int32, (16, 16), 1)
    before = dot((j1 < j0).astype(BF), count, 1, 0)
    kept = (member > 0.0) & (local + before < cap[0].astype(F32))
    rank[...] = jnp.where(kept, local, -1.0)
    wload.wait()

    def attend_cols(t, carry):
        w = part[pl.ds(2 * t, 2)].reshape(2 * rows, width)
        att[:, pl.ds(pl.multiple_of(t * 2 * rows, 2 * rows), 2 * rows)] = dot(ctx[...], w, 1, 1)
        return carry

    lax.fori_loop(0, 8, attend_cols, 0)
    n2[...] = rmsnorm(tok[...].astype(F32) + att[...], gain[...]).astype(BF)
    gn.begin()
    for c in loads:
        c.start()
    saves = []
    gc.near(1)
    gn.near(1)
    order = (1, 2, 3, 0)
    for i, k in enumerate(order):
        for g in (gn, gc):
            if i < 3:
                g.far(k)
            if i < 2:
                g.near(order[i + 1])
            if i == 2:
                g.far(0)
        gn.ready(k)
        gc.ready(k)
        if i >= 1:
            sc.near(order[i - 1])
        if i >= 2:
            sc.along(order[i - 2])
        for c in saves:
            c.wait()
        if i == 0:
            for c in loads:
                c.wait()
        if i == 3:
            sm.far(1)
            sm.far(2)

        def collect(j, carry):
            b = place_of(k, j)
            to = pl.ds(pl.multiple_of(j * SLOTS, SLOTS), SLOTS)
            s0 = lax.broadcasted_iota(jnp.int32, (SLOTS, rows), 0).astype(F32)
            mine = s0 == rank[pl.ds(b, 1), :]
            sw[to, :] = jnp.sum(jnp.where(mine, coef[pl.ds(b, 1), :], 0.0), 1, keepdims=True)
            pick[to, :] = mine.astype(BF)

            def cols(n, c):
                w = pl.ds(pl.multiple_of(n * 512, 512), 512)
                xr[to, w] = dot(pick[to, :], nall[b, :, w], 1, 0).astype(BF)
                pg[to, w] = (dot(pick[to, :], call[b, :, w], 1, 0) * sw[to, :]).astype(BF)
                return c

            return lax.fori_loop(0, width // 512, cols, carry)

        lax.fori_loop(0, 4, collect, 0)

        def inner(n, carry):
            w = pl.ds(pl.multiple_of(n * COLS, COLS), COLS)
            gate = dot(xr[...], wg[:, w], 1, 0)
            up = dot(xr[...], wu[:, w], 1, 0)
            hg = dot(pg[...], wd[w, :], 1, 1)
            sig = jax.nn.sigmoid(gate)
            hid[:, w] = (gate * sig * up).astype(BF)
            gg[:, w] = (hg * up * sig * (1.0 + gate * (1.0 - sig))).astype(BF)
            ug[:, w] = (hg * gate * sig).astype(BF)
            return carry

        lax.fori_loop(0, hid.shape[1] // COLS, inner, 0)

        def outer(n, carry):
            w = pl.ds(pl.multiple_of(n * COLS, COLS), COLS)
            eo = dot(hid[...], wd[:, w], 1, 0).astype(BF).astype(F32)
            rg = (dot(gg[...], wg[w, :], 1, 1) + dot(ug[...], wu[w, :], 1, 1)).astype(BF)
            for j in range(4):
                b = place_of(k, j)
                cut = slice(j * SLOTS, (j + 1) * SLOTS)
                weighted = (eo[cut] * sw[cut]).astype(BF)
                stage[j, :, w] = dot(pick[cut], weighted, 0, 0).astype(BF)
                part[b, :, w] = dot(pick[cut], rg[cut], 0, 0).astype(BF)
            return carry

        lax.fori_loop(0, xr.shape[1] // COLS, outer, 0)
        sc.far(k)
        saves = [
            pltpu.make_async_copy(a, o.at[k], osem.at[i])
            for i, (a, o) in enumerate([(xr, xr_o), (pg, pg_o), (hid, hid_o), (gg, gg_o), (ug, ug_o)])
        ] + [pltpu.make_async_copy(stage.at[j], p1.at[place_of(k, j)], psem.at[j]) for j in range(4)]
        for c in saves:
            c.start()
    gn.end()
    gc.end()
    sc.along(3)
    sc.near(0)
    for c in saves:
        c.wait()
    sm.far(3)
    sm.far(0)
    sc.along(0)
    sc.end()
    for c in list(sm.da.values()) + list(sm.db.values()):
        c.wait()


def expert(ctx, wout, tokens, gain, cot, meta, cap, wg, wu, wd, cid):
    rows, width = ctx.shape
    ff = wg.shape[1]
    chunk = 4 * SLOTS
    save = lambda w: jax.ShapeDtypeStruct((4, chunk, w), BF)
    v = lambda *shape: pltpu.VMEM(shape, BF)
    f = lambda *shape: pltpu.VMEM(shape, F32)
    return pl.pallas_call(
        expert_kernel,
        out_shape=[
            jax.ShapeDtypeStruct((rows, width), F32),
            jax.ShapeDtypeStruct((rows, width), F32),
            jax.ShapeDtypeStruct((16, rows, width), BF),
            jax.ShapeDtypeStruct((8, rows // 2, width), BF),
            save(width), save(width), save(ff), save(ff), save(ff),
        ],
        in_specs=[VM, ANY, VM, VM, ANY, VM, pl.BlockSpec(memory_space=pltpu.SMEM), ANY, ANY, ANY],
        out_specs=[VM, VM] + [ANY] * 7,
        scratch_shapes=[
            v(rows, width), f(16, rows), f(16, rows), v(chunk, rows), f(chunk, 1),
            v(16, rows, width), v(16, rows, width), v(16, rows, width), v(4, rows, width),
            v(width, ff), v(width, ff), v(ff, width),
            v(chunk, width), v(chunk, width), v(chunk, ff), v(chunk, ff), v(chunk, ff),
        ]
        + scatter_bufs(rows, width)
        + [pltpu.SemaphoreType.DMA, pltpu.SemaphoreType.DMA((3,)), pltpu.SemaphoreType.DMA((5,)), pltpu.SemaphoreType.DMA((4,))]
        + [pltpu.SemaphoreType.DMA((4, 2))] * 2
        + GATHER_SEMS * 2
        + SCATTER_SEMS,
        compiler_params=params(cid, 62),
        name="expert",
    )(ctx, wout, tokens, gain, cot, meta, cap, wg, wu, wd)


TILE = (256, 1024)


def weights_kernel(
    p1, rdm, xr_h, pg_h, hid_h, gg_h, ug_h, wout, n2g, tok, att, cot, gain,
    mix, gate_o, up_o, down_o, ag, mg, gain_g, cgh,
    part, wo, cg, xr, pg, hid, gg, ug, own, give, got, rd, rx, ry, rz, lsem, wsem, gs, gr, os_, cs, cr, co, *sems,
):
    me = lax.axis_index("dp")
    blk = lambda b: pl.ds(pl.multiple_of(b * HD, HD), HD)
    loads = [
        pltpu.make_async_copy(a, b, lsem.at[i])
        for i, (a, b) in enumerate(
            [(p1, part), (rdm, rd), (xr_h, xr), (gg_h, gg), (ug_h, ug), (hid_h, hid), (pg_h, pg)]
        )
    ]
    column_load = lambda t: pltpu.make_async_copy(
        wout.at[:, pl.ds(pl.multiple_of(t * 256, 256), 256)], wo.at[lax.rem(t, 2)], wsem.at[lax.rem(t, 2)]
    )
    column_load(0).start()
    for c in loads:
        c.start()
    back, gains = rmsnorm_pull(tok[...].astype(F32) + att[...], gain[...], n2g[...])
    gain_g[...] = jnp.sum(gains, 0, keepdims=True)
    mg[...] = cot[...].astype(F32) + back
    ag[...] = mg[...].astype(BF)
    barrier([lax.rem(me + d, 16) for d in range(1, 16)], pair=True)
    sc = Scatter(part, mix, part.shape[1], (rd, rx, ry, rz), sems)
    tiles = cg.shape[1] // 256

    def context_cols(t, carry):
        @pl.when(t + 1 < tiles)
        def _():
            column_load(t + 1).start()

        column_load(t).wait()
        cols = pl.ds(pl.multiple_of(t * 256, 256), 256)
        cg[:, cols] = dot(ag[...], wo[lax.rem(t, 2)], 1, 0).astype(BF)
        return carry

    lax.fori_loop(0, tiles, context_cols, 0)

    def hop(d):
        to = lax.rem(me + d, 16)
        return pltpu.make_async_remote_copy(
            src_ref=cg.at[:, blk(to)], dst_ref=cgh.at[blk(me)], send_sem=cs.at[d], recv_sem=cr.at[d],
            device_id={"dp": to}, device_id_type=MESH,
        )

    for d in range(1, 16):
        hop(d).start()
    stay = pltpu.make_async_copy(cg.at[:, blk(me)], cgh.at[blk(me)], co)
    stay.start()
    loads[0].wait()
    loads[1].wait()
    order = (1, 2, 3, 0)
    for k in order:
        sc.near(k)
    for c in loads[2:]:
        c.wait()
    r, w = TILE

    def product(m, t):
        if m < 2:
            return dot(xr[:, pl.ds(pl.multiple_of(t * r, r), r)], (gg, ug)[m][...], 0, 0)
        i, j = t // 2, t % 2
        return dot(hid[:, pl.ds(pl.multiple_of(i * r, r), r)], pg[:, pl.ds(pl.multiple_of(j * w, w), w)], 0, 0)

    def home(m, t):
        if m < 2:
            return (gate_o, up_o)[m].at[pl.ds(pl.multiple_of(t * r, r), r)]
        i, j = t // 2, t % 2
        return down_o.at[pl.ds(pl.multiple_of(i * r, r), r), pl.ds(pl.multiple_of(j * w, w), w)]

    for m in range(3):

        def sent(t, m=m):
            s = lax.rem(t, 2)
            return pltpu.make_async_remote_copy(
                src_ref=give.at[s], dst_ref=got.at[m, t], send_sem=gs.at[s], recv_sem=gr.at[m, t],
                device_id={"grp": partner()}, device_id_type=MESH,
            )

        def saved(t, m=m):
            s = lax.rem(t, 2)
            return pltpu.make_async_copy(own.at[s], home(m, t), os_.at[s])

        def finish(t, m=m):
            s = lax.rem(t, 2)
            sent(t, m).wait_recv()
            own[s] = (own[s].astype(F32) + got[m, t].astype(F32)).astype(BF)
            saved(t, m).start()

        def body(t, carry, m=m):
            s = lax.rem(t, 2)

            @pl.when(t >= 2)
            def _():
                sent(t - 2, m).wait_send()
                saved(t - 2, m).wait()

            low = product(m, t).astype(BF)
            give[s] = low
            own[s] = low
            sent(t, m).start()

            @pl.when(t >= 1)
            def _():
                finish(t - 1, m)

            return carry

        lax.fori_loop(0, 8, body, 0)
        finish(7, m)
        for t in (6, 7):
            sent(t, m).wait_send()
            saved(t, m).wait()
        if m == 0:
            sc.along(1)
        if m == 1:
            sc.along(2)
            sc.along(3)
    sc.along(0)
    sc.end()
    stay.wait()
    for d in range(1, 16):
        hop(d).wait()


def expert_weights(p1, rdm, xr, pg, hid, gg, ug, wout, n2g, tokens, att, cot, gain, cid):
    _, rows, width = p1.shape
    n, ff = gg.shape
    seq = wout.shape[0]
    r, w = TILE
    v = lambda *shape: pltpu.VMEM(shape, BF)
    sem = lambda *shape: pltpu.SemaphoreType.DMA(shape) if shape else pltpu.SemaphoreType.DMA
    b = lambda *shape: jax.ShapeDtypeStruct(shape, BF)
    f = lambda *shape: jax.ShapeDtypeStruct(shape, F32)
    return pl.pallas_call(
        weights_kernel,
        out_shape=[
            f(rows, width), b(width, ff), b(width, ff), b(ff, width), b(rows, width), f(rows, width), f(1, width),
            b(16 * rows, HD),
        ],
        in_specs=[ANY] * 8 + [VM] * 5,
        out_specs=[VM] + [ANY] * 3 + [VM] * 3 + [ANY],
        scratch_shapes=[
            v(16, rows, width), v(2, seq, 256), v(rows, width),
            v(n, width), v(n, width), v(n, ff), v(n, ff), v(n, ff), v(2, r, w), v(2, r, w), v(3, 8, r, w),
        ]
        + scatter_bufs(rows, width)
        + [sem(7), sem(2), sem(2), sem(3, 8), sem(2), sem(16), sem(16), sem()]
        + SCATTER_SEMS,
        compiler_params=params(cid, 63),
        name="expert_weights",
    )(p1, rdm, xr, pg, hid, gg, ug, wout, n2g, tokens, att, cot, gain)


def back_kernel(
    cgh, q, k, v, seg, sk, lse, cosf, sinf, wh, nall, ag, ctx,
    ngrad, out_t, qkv_t,
    dkt, dvt, pgrad, pgt, opart, opair, osum, ostage, ord_, orx, ory, orz,
    part, rd, rx, ry, rz, ntile, qpart, qpair,
    lo, ops, opr, ofs, ofr, nsem, qs, qr, ts, tr, fs, fr, *sems,
):
    me = lax.axis_index("dp")
    core = lax.axis_index("grp") % 2
    hr = HD // 2
    mine, other = pl.multiple_of(core * hr, hr), pl.multiple_of((1 - core) * hr, hr)
    blk = lambda b: pl.ds(pl.multiple_of(b * HD, HD), HD)
    barrier([lax.rem(me + d, 16) for d in range(1, 16)], pair=True)
    tiles = [
        pltpu.make_async_copy(nall.at[:, pl.ds(t * 256, 256)], ntile.at[t % 2], nsem.at[t % 2])
        for t in range(wh.shape[1] // 256)
    ]

    def out_block(b, carry):
        opart[b] = dot(ag[:, blk(b)], ctx[...], 0, 0).astype(BF)
        return carry

    lax.fori_loop(0, 16, out_block, 0)
    pair = push_pair(opart.at[:, pl.ds(other, hr)], opair, ops, opr)
    dkt[...] = jnp.zeros_like(dkt)
    dvt[...] = jnp.zeros_like(dvt)
    so = Scatter(opair, osum, hr, (ord_, orx, ory, orz), sems[:8])
    sn = Scatter(part, ngrad, HD, (rd, rx, ry, rz), sems[8:16])
    pair.wait_recv()

    def out_pair(b, carry):
        opair[b] = (opair[b].astype(F32) + opart[b, pl.ds(mine, hr)].astype(F32)).astype(BF)
        return carry

    lax.fori_loop(0, 16, out_pair, 0)
    order = (1, 2, 3, 0)
    for j in order:
        so.far(j)

    def attend_rows(i, carry):
        row = blk(i)
        s = dot(q[row], k[...], 1, 1)
        prob = jnp.where(column(seg, i) == sk[...], jnp.exp2(s * (SCALE * LOG2E) - lse[row]), 0.0)
        dp = dot(cgh[row], v[...], 1, 1)
        delta = jnp.sum(prob * dp, -1, keepdims=True)
        ds = (prob * (dp - delta)).astype(BF)
        dq = dot(ds, k[...], 1, 0) * SCALE
        dq = dq * cosf[row] - pltpu.roll(dq, HD // 2, 1) * sinf[row]
        pgrad[row, :HD] = dq.astype(BF)
        pgt[:HD, row] = dq.T.astype(BF)
        dkt[...] += dot(q[row], ds, 0, 0)
        dvt[...] += dot(cgh[row], prob.astype(BF), 0, 0)
        return carry

    n = q.shape[0] // HD
    lax.fori_loop(0, n // 2, attend_rows, 0)
    for j in order:
        so.near(j)
    lax.fori_loop(n // 2, n, attend_rows, 0)
    for j in order:
        so.along(j)

    def turn_back(i, carry):
        row = blk(i)
        dk = dkt[:, row].T * SCALE
        dk = dk * cosf[row] - pltpu.roll(dk, HD // 2, 1) * sinf[row]
        pgrad[row, HD : 2 * HD] = dk.astype(BF)
        pgt[HD : 2 * HD, row] = dk.T.astype(BF)
        dv = dvt[:, row]
        pgrad[row, 2 * HD :] = dv.T.astype(BF)
        pgt[2 * HD :, row] = dv.astype(BF)
        return carry

    lax.fori_loop(0, n, turn_back, 0)
    tiles[0].start()

    def back_block(j, kk):
        b = place_of(kk, j)
        part[b] = dot(pgrad[blk(b)], wh[...], 1, 0).astype(BF)

    for kk in order:
        back_block(3, kk)
        sn.far(kk)
    for t, c in enumerate(tiles):
        if t + 1 < len(tiles):
            tiles[t + 1].start()
        c.wait()
        qpart[:, t * 256 : (t + 1) * 256] = dot(pgt[...], ntile[t % 2], 1, 0).astype(BF)
    qc = [push_pair(qpart.at[pl.ds(s * HD + other, hr)], qpair.at[s], qs.at[s], qr.at[s]) for s in range(3)]
    so.end()
    ostage[...] = osum[...].astype(BF)
    keep = pltpu.make_async_copy(ostage, out_t.at[pl.ds(mine, hr)], lo)
    keep.start()
    give = push_pair(ostage, out_t.at[pl.ds(mine, hr)], ofs, ofr)
    for kk in order:
        back_block(1, kk)
        back_block(2, kk)
        sn.near(kk)
    for s in range(3):
        qc[s].wait_recv()
        qpair[s] = (qpair[s].astype(F32) + qpart[pl.ds(s * HD + mine, hr)].astype(F32)).astype(BF)
        b = 16 * s + me
        to, slot = b // 3, lax.rem(b, 3)
        dst = qkv_t.at[pl.ds(pl.multiple_of(slot * HD + core * hr, hr), hr)]

        @pl.when(to != me)
        def _():
            push(qpair.at[s], dst, ts.at[s], tr.at[slot], to)

        @pl.when(to == me)
        def _():
            pltpu.make_async_copy(qpair.at[s], dst, tr.at[slot]).start()

    for kk in order:
        back_block(0, kk)
    for kk in order:
        sn.along(kk)
    fc = []
    for s in range(3):
        here = qkv_t.at[pl.ds(pl.multiple_of(s * HD + core * hr, hr), hr)]
        pltpu.make_async_copy(here, here, tr.at[s]).wait()
        fc.append(push_pair(here, here, fs.at[s], fr.at[s]))
    sn.end()
    for s in range(3):

        @pl.when((16 * s + me) // 3 != me)
        def _():
            pltpu.make_async_copy(qpair.at[s], qpair.at[s], ts.at[s]).wait()

    keep.wait()
    give.wait()
    pair.wait_send()
    for c in qc:
        c.wait_send()
    for c in fc:
        c.wait()


def back(cgh, q, k, v, seg, sk, lse, cosf, sinf, wh, nall, ag, ctx, cid):
    rows, width = ag.shape
    seq = q.shape[0]
    vb = lambda *shape: pltpu.VMEM(shape, BF)
    vf = lambda *shape: pltpu.VMEM(shape, F32)
    sem = lambda *shape: pltpu.SemaphoreType.DMA(shape) if shape else pltpu.SemaphoreType.DMA
    return pl.pallas_call(
        back_kernel,
        out_shape=[
            jax.ShapeDtypeStruct((rows, width), F32),
            jax.ShapeDtypeStruct((rows, width), BF),
            jax.ShapeDtypeStruct((3 * HD, width), BF),
        ],
        in_specs=[VM] * 10 + [ANY, VM, VM],
        out_specs=[VM, ANY, ANY],
        scratch_shapes=[
            vf(HD, seq), vf(HD, seq), vb(seq, 3 * HD), vb(3 * HD, seq),
            vb(16, rows, width), vb(16, rows // 2, width), vf(rows // 2, width), vb(rows // 2, width),
        ]
        + scatter_bufs(rows // 2, width)
        + [vb(16, rows, width)]
        + scatter_bufs(rows, width)
        + [vb(2, seq, 256), vb(3 * HD, width), vb(3, HD // 2, width)]
        + [sem(), sem(), sem(), sem(), sem(), sem(2), sem(3), sem(3), sem(3), sem(3), sem(3), sem(3)]
        + SCATTER_SEMS * 2,
        compiler_params=params(cid, 62),
        name="back",
    )(cgh, q, k, v, seg, sk, lse, cosf, sinf, wh, nall, ag, ctx)


def total_kernel(x, dp_o, pair_o, got, fromp, ss, rs, ps, pr):
    me = lax.axis_index("dp")
    barrier([lax.rem(me + d, 16) for d in range(1, 16)], pair=True)
    sent = [push(x, got.at[me], ss.at[d], rs.at[d], lax.rem(me + d, 16)) for d in range(1, 16)]
    got[me] = x[...]
    for c in sent:
        c.wait_recv()
    acc = got[0]
    for j in range(1, 16):
        acc = acc + got[j]
    dp_o[...] = acc
    c = push_pair(dp_o, fromp, ps, pr)
    c.wait()
    pair_o[...] = acc + fromp[...]
    for c in sent:
        c.wait_send()


def total(x, cid):
    sem = pltpu.SemaphoreType.DMA
    return pl.pallas_call(
        total_kernel,
        out_shape=[jax.ShapeDtypeStruct(x.shape, F32)] * 2,
        in_specs=[VM],
        out_specs=[VM, VM],
        scratch_shapes=[pltpu.VMEM((16,) + x.shape, F32), pltpu.VMEM(x.shape, F32), sem((16,)), sem((16,)), sem, sem],
        compiler_params=params(cid, 16),
        name="total",
    )(x)


def rotary_tables(length):
    freq = (THETA ** (-(np.arange(HD // 2) * 2.0 / HD))).astype(np.float32)
    angle = (np.arange(length, dtype=np.float32)[:, None] * freq[None, :]).astype(np.float64)
    cos, sin = np.cos(angle).astype(np.float32), np.sin(angle).astype(np.float32)
    return np.concatenate([cos, cos], 1), np.concatenate([-sin, sin], 1)


def per_device(
    tokens, segments, routes, route_weight, capacity, norm_gain,
    qkv_weight, out_weight, gate_weight, up_weight, down_weight, cotangent,
):
    rows, width = tokens.shape
    seq = segments.shape[0]
    me = lax.axis_index("dp")
    gain1_row, gain2_row = norm_gain[:1], norm_gain[1:]
    stream = tokens.astype(F32)
    meta = jnp.concatenate([routes.astype(F32).T, route_weight.T], 0)
    seg = segments.astype(F32).reshape(16, rows)
    sk = jnp.where(segments == 0, -1.0, segments.astype(F32))[None, :]
    cos_table, sin_table = rotary_tables(seq)
    normed_all, meta_all, w_head, q, k, v, lse, context, dense_out = front(
        tokens, gain1_row, meta, qkv_weight, out_weight, cos_table, sin_table, seg, sk, 0
    )
    attended, n2g, mix_part, mix_far, xr, pg, hidden, gg, ug = expert(
        context, dense_out, tokens, gain2_row, cotangent, meta_all, capacity,
        gate_weight[0], up_weight[0], down_weight[0], 3,
    )
    flat = lambda a: a.reshape(-1, a.shape[2])
    mixture, gate_g, up_g, down_g, attended_grad, middle_grad, gain2, cgh = expert_weights(
        mix_part, mix_far, flat(xr), flat(pg), flat(hidden), flat(gg), flat(ug), flat(dense_out),
        n2g, tokens, attended, cotangent, gain2_row, 5,
    )
    layer = stream + attended + mixture
    own_seg = lax.dynamic_slice_in_dim(segments, me * rows, rows)
    valid = (own_seg != 0).astype(F32)
    sums = jnp.stack(
        [
            jnp.sum(valid * jnp.sum(layer * layer, -1)),
            jnp.sum(valid * jnp.sum(attended * attended, -1)),
            jnp.sum(valid * jnp.sum(mixture * mixture, -1)),
            jnp.sum(valid) * width,
        ]
    )
    normed_grad, out_total, qkv_total = back(
        cgh, q, k, v, seg, sk, lse, cos_table, sin_table, w_head, flat(normed_all), attended_grad, context, 6
    )
    sg, gain1 = rmsnorm_pull(stream, gain1_row, normed_grad)
    tokens_grad = middle_grad + sg
    small = jnp.concatenate([jnp.sum(gain1, 0), gain2[0], sums, jnp.zeros((1024 - sums.size,), F32)]).reshape(-1, HD)
    in_group, in_pair = total(small, 4)
    seq_sums = in_group.reshape(-1)[2 * width : 2 * width + 4]
    gain_pair = in_pair.reshape(-1)[: 2 * width].reshape(2, width)
    stat_row = jnp.sqrt(seq_sums[:3] / seq_sums[3]).reshape(1, 3)
    groups = lax.axis_size("grp")
    over = lambda a: a.astype(F32) if groups == 2 else lax.psum(a.astype(BF), "grp").astype(F32) * 0.5
    return (
        layer.astype(BF),
        tokens_grad,
        over(qkv_total),
        over(out_total),
        over(gate_g)[None],
        over(up_g)[None],
        over(down_g)[None],
        gain_pair if groups == 2 else lax.psum(gain_pair, "grp") * 0.5,
        stat_row,
    )


def solution(mesh):
    both = ("grp", "dp")
    in_specs = (
        P(both, None), P("grp"), P(both, None), P(both, None), P(), P(),
        P("dp", None), P("dp", None), P("dp", None, None), P("dp", None, None), P("dp", None, None),
        P(both, None),
    )
    out_specs = (
        P(both, None), P(both, None), P("dp", None), P("dp", None),
        P("dp", None, None), P("dp", None, None), P("dp", None, None), P(), P("grp", None),
    )
    return jax.shard_map(per_device, mesh=mesh, in_specs=in_specs, out_specs=out_specs, check_vma=False)
```

profile of v0, /device:TPU:5, one launch (start us, length us, event | category | flops | bytes accessed | tf_op | source)
XLA Modules:
  0.0 731.7 jit_solution(14738347504603558135)
XLA Ops:
  0.6 1.4 fusion.11
  2.0 1.4 convert_select_fusion
  3.4 1.3 convert_bitcast_fusion.seg
  4.7 0.7 convert_bitcast_fusion.1
  5.4 1.3 pad_maximum_fusion.m_ref
  6.7 158.7 %front.1 = (bf16[16,128,2048]{2,1,0:T(8,128)(2,1)}, f32[16,16,128]{2,1,0:T(8,128)}, bf16[384,2048]{1,0:T(8,128)(2,1)}, bf16[2048,128]{1,0:T(8,128)(2,1)}, bf16[2...) custom-call(bf16[128,2048]{1,0:T(8,128)(2,1)} %tok.5, ...), custom_call_target="tpu_custom_call" | custom-call | tf_op jit(solution)/shard_map/front/pallas_call | solution.py:375
  166.0 260.4 %expert.1 = (f32[128,2048]{1,0:T(8,128)}, f32[128,2048]{1,0:T(8,128)}, bf16[16,128,2048]{2,1,0:T(8,128)(2,1)}, bf16[8,64,2048]{2,1,0:T(8,128)(2,1)}, bf16[4,320,...) custom-call(bf16[128,2048]{1,0:T(8,128)(2,1)} %get-tuple-element.40., ...), custom_call_target="tpu_custom_call" | custom-call | tf_op jit(solution)/shard_map/expert/pallas_call | solution.py:544
  426.4 91.0 %expert_weights.1 = (f32[128,2048]{1,0:T(8,128)}, bf16[2048,1024]{1,0:T(8,128)(2,1)}, bf16[2048,1024]{1,0:T(8,128)(2,1)}, bf16[1024,2048]{1,0:T(8,128)(2,1)}, bf...) custom-call(bf16[16,128,2048]{2,1,0:T(8,128)(2,1)} %get-tuple-element.44.p1, ...), custom_call_target="tpu_custom_call" | custom-call | tf_op jit(solution)/shard_map/expert_weights/pallas_call | solution.py:709
  517.4 0.0 copy-start
  517.4 0.0 copy-start.2
  517.4 0.0 copy-start.7
  517.5 159.5 %back.1 = (f32[128,2048]{1,0:T(8,128)}, bf16[128,2048]{1,0:T(8,128)(2,1)}, bf16[384,2048]{1,0:T(8,128)(2,1)}) custom-call(bf16[2048,128]{1,0:T(8,128)(2,1)} %get-tuple-element.54.cgh, bf16[2048,128]{1,0:T(8,128)(2,1)} %get-tuple-element.55.q, bf16[2048,128]{1,0:T(8,128)(2,1)} %get-tuple-element.56.k, bf16[2048,128]{1,0:T(8,128)(2,1)} %get-tuple-element.57.v, ...), custom_call_target="tpu_custom_call" | custom-call | tf_op jit(solution)/shard_map/back/pallas_call | solution.py:873
  677.0 0.0 copy-start.8
  677.0 0.0 copy-done
  677.0 0.0 copy-done.2
  677.0 2.4 multiply_reduce_fusion
  679.5 0.0 copy-done.7
  679.5 1.5 fusion.6
  681.0 1.4 convert_reduce_fusion
  683.0 0.0 copy-done.8
  683.0 2.0 concatenate.7
  685.0 23.2 %total.1 = (f32[40,128]{1,0:T(8,128)S(1)}, f32[40,128]{1,0:T(8,128)S(1)}) custom-call(f32[40,128]{1,0:T(8,128)S(1)} %bitcast.36), custom_call_target="tpu_custom_call" | custom-call | tf_op jit(solution)/shard_map/total/pallas_call | solution.py:917
  708.3 0.6 slice.25
  708.9 1.2 fusion.10
  710.0 0.6 reshape.86
  710.7 0.0 copy-start.1
  710.7 11.9 %bitcast_convert_fusion.1 = (f32[1,2048,1024]{2,1,0:T(8,128)}, f32[1,2048,1024]{2,1,0:T(8,128)}) fusion(bf16[2048,1024]{1,0:T(8,128)(2,1)} %get-tuple-element.66, bf16[2048,1024]{1,0:T(8,128)(2,1)} %get-tuple-element.65), kind=kLoop, calls=%fused_computation.1 | loop fusion | flops 4194304 | bytes 25165824 | tf_op jit(solution)/shard_map/broadcast_in_dim | solution.py:989
  722.6 0.0 copy-done.1
  722.6 0.0 copy-start.4
  722.6 4.4 bitcast_convert_fusion
  727.0 0.0 copy-start.3
  727.0 0.0 copy-start.5
  727.0 0.0 copy-done.4
  727.0 0.0 copy-start.6
  727.0 2.0 convert_element_type.29
  729.1 0.0 copy-done.3
  729.1 0.1 copy-done.5
  729.1 1.3 fusion.4
  730.4 0.0 copy-done.6
  730.4 1.1 convert_element_type.30
  (3 shorter events, 0.0 us)
Async XLA Ops:
  517.4 159.6 %copy-start = (bf16[128,2048]{1,0:T(8,128)(2,1)S(1)}, bf16[128,2048]{1,0:T(8,128)(2,1)}, u32[]{:S(2)}) copy-start(bf16[128,2048]{1,0:T(8,128)(2,1)} %tok.5) | copy-start | bytes 1572868
  517.4 159.6 %copy-start.2 = (f32[128,2048]{1,0:T(8,128)S(1)}, f32[128,2048]{1,0:T(8,128)}, u32[]{:S(2)}) copy-start(f32[128,2048]{1,0:T(8,128)} %get-tuple-element.43.att) | copy-start | bytes 3145732
  517.4 162.0 %copy-start.7 = (f32[1,2048]{1,0:T(1,128)S(1)}, f32[1,2048]{1,0:T(1,128)}, u32[]{:S(2)}) copy-start(f32[1,2048]{1,0:T(1,128)} %get-tuple-element.83.gain) | copy-start | bytes 24580
  677.0 6.0 copy-start.8
  710.7 11.9 %copy-start.1 = (bf16[1024,2048]{1,0:T(8,128)(2,1)S(1)}, bf16[1024,2048]{1,0:T(8,128)(2,1)}, u32[]{:S(2)}) copy-start(bf16[1024,2048]{1,0:T(8,128)(2,1)} %get-tuple-element.67) | copy-start | bytes 12582916
  722.6 4.5 copy-start.4
  727.0 2.0 copy-start.3
  727.0 2.1 copy-start.5
  727.0 3.4 copy-start.6
where the time goes:
time: 743 us; the launch traced here: 732 us
  Pallas kernels  693 us (93%)
  other arithmetic  31.9 us (4%)
    pallas_call x1, Pallas kernels, expert(): pl.pallas_call(expert_kernel, out_shape=[jax.ShapeDtypeStruct((rows, widt...  260 us
    pallas_call x1, Pallas kernels, back(): pl.pallas_call(back_kernel, out_shape=[jax.ShapeDtypeStruct((rows, width)...  160 us
    pallas_call x1, Pallas kernels, front(): pl.pallas_call(front_kernel, out_shape=[b(16, rows, width), f(16, *meta.s...  159 us
    pallas_call x1, Pallas kernels, expert_weights(): pl.pallas_call(weights_kernel, out_shape=[f(rows, width), b(width, ff), b...  91 us
    pallas_call x1, Pallas kernels, total(): pl.pallas_call(total_kernel, out_shape=[jax.ShapeDtypeStruct(x.shape, F32...  23.2 us

commit v1 on v0

--- a/solution.py
+++ b/solution.py
@@ -69,7 +69,11 @@
     return c
 
 
-GATHER_SEMS = [pltpu.SemaphoreType.DMA((4,))] * 6 + [pltpu.SemaphoreType.DMA((4, 2))] * 2 + [pltpu.SemaphoreType.DMA]
+ORDER = (1, 0, 3, 2)
+GATHER_SEMS = (
+    [pltpu.SemaphoreType.DMA((4,))] * 6 + [pltpu.SemaphoreType.DMA((4, 2))] * 2 + [pltpu.SemaphoreType.DMA]
+    + [pltpu.SemaphoreType.DMA((4,))] * 2
+)
 
 
 class Gather:
@@ -84,7 +88,7 @@
         return self.dst.at[b, pl.ds(self.first + h * half, half)]
 
     def begin(self):
-        zs, zr, xs, xr, ys, yr, _, _, own = self.sems
+        zs, zr, xs, xr, ys, yr, _, _, own, _, _ = self.sems
         p, src = self.p, self.src
         me = p["me"]
         self.mine = pltpu.make_async_copy(src, self.block(me), own)
@@ -92,10 +96,10 @@
         self.xc = {0: push(src, self.block(me), xs.at[0], xr.at[0], p["X"][0])}
         self.yc = {0: push(src, self.block(me), ys.at[0], yr.at[0], p["Y"][0])}
         self.zc = {k: push(src, self.block(me), zs.at[k], zr.at[k], p["col"][k]) for k in (1, 2, 3)}
-        self.dc = {}
+        self.dc, self.vc = {}, {}
 
     def near(self, k):
-        _, _, xs, xr, ys, yr, _, _, _ = self.sems
+        _, _, xs, xr, ys, yr = self.sems[:6]
         p = self.p
         self.zc[k].wait_recv()
         b = self.block(p["col"][k])
@@ -112,28 +116,25 @@
         self.yc[k].wait_recv()
         self.dc[k, 1] = push(b, b, ds.at[k, 1], dr.at[k, 1], p["X"][0])
 
-    def step(self, k):
-        self.far(k)
-        if k < 3:
-            self.near(k + 1)
+    def over(self, k):
+        vs, vr = self.sems[9:11]
+        self.dc[k, 0].wait_recv()
+        self.dc[k, 1].wait_recv()
+        b = self.block(self.p["D"][k])
+        self.vc[k] = push(b, b, vs.at[k], vr.at[k], self.p["col"][1])
 
     def ready(self, k):
         if k == 0:
             self.mine.wait()
-        self.dc[k, 0].wait_recv()
-        self.dc[k, 1].wait_recv()
+        if k % 2:
+            self.xc[k].wait_recv()
+            self.yc[k].wait_recv()
+            self.vc[k - 1].wait_recv()
 
     def end(self):
-        for group in (self.xc, self.yc, self.zc, self.dc):
+        for group in (self.xc, self.yc, self.zc, self.dc, self.vc):
             for c in group.values():
                 c.wait_send()
-
-    def all(self):
-        for k in range(4):
-            self.step(k)
-        for k in range(4):
-            self.ready(k)
-        self.end()
 
 
 def gather_targets():
@@ -141,48 +142,55 @@
     return [p["col"][1], p["col"][2], p["col"][3], p["X"][0], p["Y"][0]]
 
 
-SCATTER_SEMS = [pltpu.SemaphoreType.DMA((4, 2))] * 2 + [pltpu.SemaphoreType.DMA((4,))] * 6
+SCATTER_SEMS = [pltpu.SemaphoreType.DMA((4, 2))] * 2 + [pltpu.SemaphoreType.DMA((4,))] * 8
 
 
 def scatter_bufs(rows, width):
     return [
-        pltpu.VMEM((8, rows // 2, width), BF),
+        pltpu.VMEM((4, rows // 2, width), BF),
         pltpu.VMEM((4, rows, width), BF),
         pltpu.VMEM((4, rows, width), BF),
         pltpu.VMEM((4, rows, width), BF),
+        pltpu.VMEM((2, rows, width), BF),
     ]
 
 
 class Scatter:
     def __init__(self, part, out, rows, bufs, sems):
         self.part, self.out, self.half, self.bufs, self.sems, self.p = part, out, rows // 2, bufs, sems, places()
-        self.da, self.db, self.xc, self.yc, self.zc = {}, {}, {}, {}, {}
+        self.da, self.db, self.xc, self.yc, self.zc, self.vc = {}, {}, {}, {}, {}, {}
+
+    def lift(self, k):
+        vs, vr = self.sems[8:]
+        self.vc[k] = push(self.part.at[self.p["D"][k]], self.bufs[4].at[k // 2], vs.at[k], vr.at[k], self.p["col"][1])
 
     def far(self, k):
         ds, dr = self.sems[:2]
-        rd, h, p = self.bufs[0], self.half, self.p
+        rd, h, p, part = self.bufs[0], self.half, self.p, self.part
         b = p["D"][k]
-        self.da[k] = push(self.part.at[b, pl.ds(0, h)], rd.at[2 * k], ds.at[k, 0], dr.at[k, 0], p["Y"][0])
-        self.db[k] = push(self.part.at[b, pl.ds(h, h)], rd.at[2 * k + 1], ds.at[k, 1], dr.at[k, 1], p["X"][0])
+        self.vc[k + 1].wait_recv()
+        part[b] = (part[b].astype(F32) + self.bufs[4][k // 2].astype(F32)).astype(BF)
+        self.da[k] = push(part.at[b, pl.ds(0, h)], rd.at[k], ds.at[k, 0], dr.at[k, 0], p["Y"][0])
+        self.db[k] = push(part.at[b, pl.ds(h, h)], rd.at[k + 1], ds.at[k, 1], dr.at[k, 1], p["X"][0])
 
     def near(self, k):
-        _, _, xs, xr, ys, yr, _, _ = self.sems
-        rd, rx, ry, _ = self.bufs
+        xs, xr, ys, yr = self.sems[2:6]
+        rd, rx, ry = self.bufs[:3]
         part, h, p = self.part, self.half, self.p
         b = p["X"][k]
-        if k in self.da:
+        if k % 2 == 0:
             self.da[k].wait_recv()
-        part[b, pl.ds(0, h)] = (part[b, pl.ds(0, h)].astype(F32) + rd[2 * k].astype(F32)).astype(BF)
+            part[b, pl.ds(0, h)] = (part[b, pl.ds(0, h)].astype(F32) + rd[k].astype(F32)).astype(BF)
         self.xc[k] = push(part.at[b], rx.at[k], xs.at[k], xr.at[k], p["X"][0])
         b = p["Y"][k]
-        if k in self.db:
+        if k % 2 == 0:
             self.db[k].wait_recv()
-        part[b, pl.ds(h, h)] = (part[b, pl.ds(h, h)].astype(F32) + rd[2 * k + 1].astype(F32)).astype(BF)
+            part[b, pl.ds(h, h)] = (part[b, pl.ds(h, h)].astype(F32) + rd[k + 1].astype(F32)).astype(BF)
         self.yc[k] = push(part.at[b], ry.at[k], ys.at[k], yr.at[k], p["Y"][0])
 
     def along(self, k):
-        zs, zr = self.sems[6:]
-        _, rx, ry, rz = self.bufs
+        zs, zr = self.sems[6:8]
+        rx, ry, rz = self.bufs[1:4]
         part = self.part
         b = self.p["col"][k]
         self.xc[k].wait_recv()
@@ -198,19 +206,38 @@
         for k in (1, 2, 3):
             self.zc[k].wait_recv()
             self.out[...] += self.bufs[3][k].astype(F32)
-        for group in (self.da, self.db, self.xc, self.yc, self.zc):
+        for group in (self.da, self.db, self.xc, self.yc, self.zc, self.vc):
             for c in group.values():
                 c.wait_send()
 
-    def all(self):
-        order = (1, 2, 3, 0)
-        for k in order:
-            self.far(k)
-        for k in order:
-            self.near(k)
-        for k in order:
-            self.along(k)
-        self.end()
+
+class PlainScatter(Scatter):
+    def far(self, k):
+        ds, dr = self.sems[:2]
+        rd, h, p = self.bufs[0], self.half, self.p
+        b = p["D"][k]
+        self.da[k] = push(self.part.at[b, pl.ds(0, h)], rd.at[2 * k], ds.at[k, 0], dr.at[k, 0], p["Y"][0])
+        self.db[k] = push(self.part.at[b, pl.ds(h, h)], rd.at[2 * k + 1], ds.at[k, 1], dr.at[k, 1], p["X"][0])
+
+    def near(self, k):
+        xs, xr, ys, yr = self.sems[2:6]
+        rd, rx, ry = self.bufs[:3]
+        part, h, p = self.part, self.half, self.p
+        b = p["X"][k]
+        self.da[k].wait_recv()
+        part[b, pl.ds(0, h)] = (part[b, pl.ds(0, h)].astype(F32) + rd[2 * k].astype(F32)).astype(BF)
+        self.xc[k] = push(part.at[b], rx.at[k], xs.at[k], xr.at[k], p["X"][0])
+        b = p["Y"][k]
+        self.db[k].wait_recv()
+        part[b, pl.ds(h, h)] = (part[b, pl.ds(h, h)].astype(F32) + rd[2 * k + 1].astype(F32)).astype(BF)
+        self.yc[k] = push(part.at[b], ry.at[k], ys.at[k], yr.at[k], p["Y"][0])
+
+
+def plain_bufs(rows, width):
+    return [pltpu.VMEM((8, rows // 2, width), BF)] + scatter_bufs(rows, width)[1:4]
+
+
+FAR_FIRST = (3, 2, 1, 0)
 
 
 ANY = pl.BlockSpec(memory_space=pl.ANY)
@@ -252,8 +279,8 @@
     half = lambda s, c: pl.ds(pl.multiple_of(s * HD + c * hr, hr), hr)
     n_ref[...] = rmsnorm(tok[...].astype(F32), gain[...]).astype(BF)
     barrier([lax.rem(me + d, 16) for d in range(1, 16)], pair=True)
-    g = Gather(n_ref, nall, n_ref.shape[0], sems[:9])
-    go = Gather(o_ref.at[half(0, core)], oall, hr, sems[9:], pl.multiple_of(core * hr, hr))
+    g = Gather(n_ref, nall, n_ref.shape[0], sems[:11])
+    go = Gather(o_ref.at[half(0, core)], oall, hr, sems[11:], pl.multiple_of(core * hr, hr))
     g.begin()
     own = pltpu.make_async_copy(m_ref, mall.at[me], mo)
     own.start()
@@ -283,25 +310,29 @@
     def project_plane(c):
         lax.fori_loop(0, 4, lambda j, carry: project(place_of(c, j), carry), 0)
 
-    for c in range(4):
-        g.step(c)
-        if c == WAIT_AT:
-            pc = []
-            for s in range(3):
-                dst = wh.at[half(s, core)]
-                pltpu.make_async_copy(dst, dst, wr.at[s]).wait()
-                pc.append(push_pair(dst, dst, ps.at[s], pr.at[s]))
-        if c == BEGIN_AT:
-            go.begin()
-        if c == WAIT_AT:
-            for p in pc:
-                p.wait_recv()
-        g.ready(c)
-        if c == WAIT_AT:
-            for e in range(c):
-                project_plane(e)
-        if c >= WAIT_AT:
-            project_plane(c)
+    g.near(1)
+    g.far(0)
+    g.near(2)
+    g.over(0)
+    g.far(2)
+    g.near(3)
+    pc = []
+    for s in range(3):
+        dst = wh.at[half(s, core)]
+        pltpu.make_async_copy(dst, dst, wr.at[s]).wait()
+        pc.append(push_pair(dst, dst, ps.at[s], pr.at[s]))
+    go.begin()
+    for p in pc:
+        p.wait_recv()
+    g.ready(0)
+    project_plane(0)
+    g.ready(1)
+    project_plane(1)
+    g.over(2)
+    g.ready(2)
+    project_plane(2)
+    g.ready(3)
+    project_plane(3)
     saves = [pltpu.make_async_copy(nall, nall_o, no), pltpu.make_async_copy(wh, wh_o, wo)]
     for c in saves:
         c.start()
@@ -332,17 +363,29 @@
         return carry
 
     lax.fori_loop(1, 8, attend_send, 0)
-    go.step(0)
+    go.near(1)
+    go.far(0)
+    go.near(2)
     lax.fori_loop(8, 16, attend_send, 0)
     attend_rows(0, 0)
     stay = pltpu.make_async_copy(ctxh.at[blk(me)], ctx.at[:, blk(me)], co)
     stay.start()
-    for c in (1, 2, 3):
-        go.step(c)
-    for c in range(4):
+    oc = []
+
+    def swap_plane(c):
         go.ready(c)
-    here = oall.at[:, pl.ds(pl.multiple_of(core * hr, hr), hr)]
-    oc = push_pair(here, here, os_, or_)
+        z = place_of(c, 0) // 4
+        here = oall.at[pl.ds(4 * z, 4), pl.ds(pl.multiple_of(core * hr, hr), hr)]
+        oc.append(push_pair(here, here, os_.at[c], or_.at[c]))
+
+    go.over(0)
+    go.far(2)
+    go.near(3)
+    swap_plane(0)
+    swap_plane(1)
+    go.over(2)
+    swap_plane(2)
+    swap_plane(3)
     g.end()
     go.end()
     own.wait()
@@ -362,7 +405,8 @@
     stay.wait()
     for d in range(1, 16):
         hop(d).wait()
-    oc.wait()
+    for c in oc:
+        c.wait()
 
 
 def front(tokens, gain, meta, w, wo, cosf, sinf, seg, sk, cid):
@@ -382,7 +426,7 @@
         out_specs=[ANY] * 3 + [VM] * 4 + [ANY] * 2,
         scratch_shapes=[v(rows, width), v(16, rows, width), v(3 * HD, width), v(seq, HD)]
         + [sem(16), sem(16), sem(), sem(3), sem(3), sem(3), sem(3), sem(), sem()]
-        + [sem(16), sem(16), sem(), sem(), sem()]
+        + [sem(16), sem(16), sem(), sem(4), sem(4)]
         + GATHER_SEMS * 2,
         compiler_params=params(cid),
         name="front",
@@ -390,8 +434,6 @@
 
 
 SLOTS = 80
-WAIT_AT = 2
-BEGIN_AT = 2
 COLS = 512
 
 
@@ -405,18 +447,17 @@
 
 def expert_kernel(
     ctx, wout, tok, gain, cot, meta, cap, wg_h, wu_h, wd_h,
-    att, n2g, p1, rdm, xr_o, pg_o, hid_o, gg_o, ug_o,
-    n2, rank, coef, pick, sw, nall, call, part, stage, wg, wu, wd, xr, pg, hid, gg, ug, rd, rx, ry, rz,
-    wosem, wsem, osem, psem, ms, mr, *sems,
+    att, n2g, p1, xr_o, pg_o, hid_o, gg_o, ug_o,
+    n2, rank, coef, pick, sw, nall, call, part, stage, wg, wu, wd, xr, pg, hid, gg, ug, rd, rx, ry, rz, rv,
+    wosem, wsem, osem, psem, *sems,
 ):
     rows, width = ctx.shape
     wload = pltpu.make_async_copy(wout, part, wosem)
     wload.start()
     barrier(gather_targets())
-    gn = Gather(n2, nall, rows, sems[:9])
-    gc = Gather(cot, call, rows, sems[9:18])
-    sc = Scatter(part, n2g, rows, (rd, rx, ry, rz), sems[18:])
-    sm = Scatter(p1, None, rows, (rdm, None, None, None), (ms, mr))
+    gn = Gather(n2, nall, rows, sems[:11])
+    gc = Gather(cot, call, rows, sems[11:22])
+    sc = Scatter(part, n2g, rows, (rd, rx, ry, rz, rv), sems[22:])
     gc.begin()
     loads = [pltpu.make_async_copy(a, b, wsem.at[i]) for i, (a, b) in enumerate([(wg_h, wg), (wu_h, wu), (wd_h, wd)])]
     me = lax.axis_index("dp").astype(F32)
@@ -443,31 +484,30 @@
     for c in loads:
         c.start()
     saves = []
-    gc.near(1)
-    gn.near(1)
-    order = (1, 2, 3, 0)
-    for i, k in enumerate(order):
-        for g in (gn, gc):
-            if i < 3:
-                g.far(k)
-            if i < 2:
-                g.near(order[i + 1])
-            if i == 2:
-                g.far(0)
-        gn.ready(k)
-        gc.ready(k)
-        if i >= 1:
-            sc.near(order[i - 1])
-        if i >= 2:
-            sc.along(order[i - 2])
+    both = lambda name, k: [getattr(g, name)(k) for g in (gn, gc)]
+    both("near", 1)
+    both("far", 0)
+    both("near", 2)
+    both("over", 0)
+    for i, k in enumerate(ORDER):
+        both("ready", k)
+        if k == 1:
+            both("far", 2)
+            both("near", 3)
+        if k == 0:
+            sc.near(1)
+            both("over", 2)
+        if k == 3:
+            sc.near(0)
+            sc.along(1)
+        if k == 2:
+            sc.near(3)
+            sc.along(0)
         for c in saves:
             c.wait()
         if i == 0:
             for c in loads:
                 c.wait()
-        if i == 3:
-            sm.far(1)
-            sm.far(2)
 
         def collect(j, carry):
             b = place_of(k, j)
@@ -513,7 +553,10 @@
             return carry
 
         lax.fori_loop(0, xr.shape[1] // COLS, outer, 0)
-        sc.far(k)
+        if k % 2:
+            sc.lift(k)
+        else:
+            sc.far(k)
         saves = [
             pltpu.make_async_copy(a, o.at[k], osem.at[i])
             for i, (a, o) in enumerate([(xr, xr_o), (pg, pg_o), (hid, hid_o), (gg, gg_o), (ug, ug_o)])
@@ -522,15 +565,11 @@
             c.start()
     gn.end()
     gc.end()
+    sc.near(2)
     sc.along(3)
-    sc.near(0)
+    sc.along(2)
+    sc.end()
     for c in saves:
-        c.wait()
-    sm.far(3)
-    sm.far(0)
-    sc.along(0)
-    sc.end()
-    for c in list(sm.da.values()) + list(sm.db.values()):
         c.wait()
 
 
@@ -547,11 +586,10 @@
             jax.ShapeDtypeStruct((rows, width), F32),
             jax.ShapeDtypeStruct((rows, width), F32),
             jax.ShapeDtypeStruct((16, rows, width), BF),
-            jax.ShapeDtypeStruct((8, rows // 2, width), BF),
             save(width), save(width), save(ff), save(ff), save(ff),
         ],
         in_specs=[VM, ANY, VM, VM, ANY, VM, pl.BlockSpec(memory_space=pltpu.SMEM), ANY, ANY, ANY],
-        out_specs=[VM, VM] + [ANY] * 7,
+        out_specs=[VM, VM] + [ANY] * 6,
         scratch_shapes=[
             v(rows, width), f(16, rows), f(16, rows), v(chunk, rows), f(chunk, 1),
             v(16, rows, width), v(16, rows, width), v(16, rows, width), v(4, rows, width),
@@ -560,7 +598,6 @@
         ]
         + scatter_bufs(rows, width)
         + [pltpu.SemaphoreType.DMA, pltpu.SemaphoreType.DMA((3,)), pltpu.SemaphoreType.DMA((5,)), pltpu.SemaphoreType.DMA((4,))]
-        + [pltpu.SemaphoreType.DMA((4, 2))] * 2
         + GATHER_SEMS * 2
         + SCATTER_SEMS,
         compiler_params=params(cid, 62),
@@ -572,31 +609,44 @@
 
 
 def weights_kernel(
-    p1, rdm, xr_h, pg_h, hid_h, gg_h, ug_h, wout, n2g, tok, att, cot, gain,
+    p1, xr_h, pg_h, hid_h, gg_h, ug_h, wout, n2g, tok, att, cot, gain,
     mix, gate_o, up_o, down_o, ag, mg, gain_g, cgh,
-    part, wo, cg, xr, pg, hid, gg, ug, own, give, got, rd, rx, ry, rz, lsem, wsem, gs, gr, os_, cs, cr, co, *sems,
+    part, wo, cg, xr, pg, hid, gg, ug, give, got, rd, rx, ry, rz, rv, lsem, wsem, gs, gr, os_, cs, cr, co, *sems,
 ):
     me = lax.axis_index("dp")
     blk = lambda b: pl.ds(pl.multiple_of(b * HD, HD), HD)
     loads = [
         pltpu.make_async_copy(a, b, lsem.at[i])
         for i, (a, b) in enumerate(
-            [(p1, part), (rdm, rd), (xr_h, xr), (gg_h, gg), (ug_h, ug), (hid_h, hid), (pg_h, pg)]
+            [(p1, part), (xr_h, xr), (gg_h, gg), (ug_h, ug), (hid_h, hid), (pg_h, pg)]
         )
     ]
     column_load = lambda t: pltpu.make_async_copy(
-        wout.at[:, pl.ds(pl.multiple_of(t * 256, 256), 256)], wo.at[lax.rem(t, 2)], wsem.at[lax.rem(t, 2)]
+        wout.at[:, pl.ds(pl.multiple_of(t * HD, HD), HD)], wo.at[lax.rem(t, 2)], wsem.at[lax.rem(t, 2)]
     )
     column_load(0).start()
     for c in loads:
         c.start()
-    back, gains = rmsnorm_pull(tok[...].astype(F32) + att[...], gain[...], n2g[...])
-    gain_g[...] = jnp.sum(gains, 0, keepdims=True)
-    mg[...] = cot[...].astype(F32) + back
-    ag[...] = mg[...].astype(BF)
+    gain_g[...] = jnp.zeros_like(gain_g)
+
+    def middle_rows(i, carry):
+        rows = pl.ds(pl.multiple_of(i * 16, 16), 16)
+        back, gains = rmsnorm_pull(tok[rows].astype(F32) + att[rows], gain[...], n2g[rows])
+        gain_g[...] += jnp.sum(gains, 0, keepdims=True)
+        grad = cot[rows].astype(F32) + back
+        mg[rows] = grad
+        ag[rows] = grad.astype(BF)
+        return carry
+
+    lax.fori_loop(0, tok.shape[0] // 16, middle_rows, 0)
     barrier([lax.rem(me + d, 16) for d in range(1, 16)], pair=True)
-    sc = Scatter(part, mix, part.shape[1], (rd, rx, ry, rz), sems)
-    tiles = cg.shape[1] // 256
+    sc = Scatter(part, mix, part.shape[1], (rd, rx, ry, rz, rv), sems)
+    loads[0].wait()
+    sc.lift(1)
+    sc.lift(3)
+    sc.near(3)
+    sc.near(1)
+    tiles = cg.shape[1] // HD
 
     def context_cols(t, carry):
         @pl.when(t + 1 < tiles)
@@ -604,7 +654,7 @@
             column_load(t + 1).start()
 
         column_load(t).wait()
-        cols = pl.ds(pl.multiple_of(t * 256, 256), 256)
+        cols = pl.ds(pl.multiple_of(t * HD, HD), HD)
         cg[:, cols] = dot(ag[...], wo[lax.rem(t, 2)], 1, 0).astype(BF)
         return carry
 
@@ -621,75 +671,77 @@
         hop(d).start()
     stay = pltpu.make_async_copy(cg.at[:, blk(me)], cgh.at[blk(me)], co)
     stay.start()
-    loads[0].wait()
-    loads[1].wait()
-    order = (1, 2, 3, 0)
-    for k in order:
-        sc.near(k)
-    for c in loads[2:]:
+    sc.far(2)
+    sc.far(0)
+    for c in loads[1:]:
         c.wait()
     r, w = TILE
+    strip = lambda a, t, size: a[:, pl.ds(pl.multiple_of(t * size, size), size)]
 
     def product(m, t):
-        if m < 2:
-            return dot(xr[:, pl.ds(pl.multiple_of(t * r, r), r)], (gg, ug)[m][...], 0, 0)
-        i, j = t // 2, t % 2
-        return dot(hid[:, pl.ds(pl.multiple_of(i * r, r), r)], pg[:, pl.ds(pl.multiple_of(j * w, w), w)], 0, 0)
-
-    def home(m, t):
-        if m < 2:
-            return (gate_o, up_o)[m].at[pl.ds(pl.multiple_of(t * r, r), r)]
-        i, j = t // 2, t % 2
-        return down_o.at[pl.ds(pl.multiple_of(i * r, r), r), pl.ds(pl.multiple_of(j * w, w), w)]
-
-    for m in range(3):
-
-        def sent(t, m=m):
+        left = strip((xr, hid)[m], t, r).T
+        for e in range(2):
+            yield dot(left, (gg, ug)[e][...] if m == 0 else pg[:, e * w : (e + 1) * w], 1, 0)
+
+    def home(m, t, e):
+        rows = pl.ds(pl.multiple_of(t * r, r), r)
+        return (gate_o, up_o)[e].at[rows] if m == 0 else down_o.at[rows, pl.ds(e * w, w)]
+
+    def sent(m, t):
+        s = lax.rem(t, 2)
+        return pltpu.make_async_remote_copy(
+            src_ref=give.at[s], dst_ref=got.at[8 * m + t], send_sem=gs.at[s], recv_sem=gr.at[8 * m + t],
+            device_id={"grp": partner()}, device_id_type=MESH,
+        )
+
+    def saved(m, t):
+        s = lax.rem(t, 2)
+        return [pltpu.make_async_copy(got.at[8 * m + t, e], home(m, t, e), os_.at[s, e]) for e in range(2)]
+
+    def finish(m, t):
+        s = lax.rem(t, 2)
+        sent(m, t).wait_recv()
+        got[8 * m + t] = (give[s].astype(F32) + got[8 * m + t].astype(F32)).astype(BF)
+        for c in saved(m, t):
+            c.start()
+
+    def free(m, t):
+        sent(m, t).wait_send()
+        for c in saved(m, t):
+            c.wait()
+
+    def body(m, start):
+        def step(t, carry):
             s = lax.rem(t, 2)
-            return pltpu.make_async_remote_copy(
-                src_ref=give.at[s], dst_ref=got.at[m, t], send_sem=gs.at[s], recv_sem=gr.at[m, t],
-                device_id={"grp": partner()}, device_id_type=MESH,
-            )
-
-        def saved(t, m=m):
-            s = lax.rem(t, 2)
-            return pltpu.make_async_copy(own.at[s], home(m, t), os_.at[s])
-
-        def finish(t, m=m):
-            s = lax.rem(t, 2)
-            sent(t, m).wait_recv()
-            own[s] = (own[s].astype(F32) + got[m, t].astype(F32)).astype(BF)
-            saved(t, m).start()
-
-        def body(t, carry, m=m):
-            s = lax.rem(t, 2)
-
-            @pl.when(t >= 2)
+
+            @pl.when(t >= start + 2)
             def _():
-                sent(t - 2, m).wait_send()
-                saved(t - 2, m).wait()
-
-            low = product(m, t).astype(BF)
-            give[s] = low
-            own[s] = low
-            sent(t, m).start()
-
-            @pl.when(t >= 1)
+                free(m, t - 2)
+
+            for e, tile in enumerate(product(m, t)):
+                give[s, e] = tile.astype(BF)
+            sent(m, t).start()
+
+            @pl.when(t >= start + 1)
             def _():
-                finish(t - 1, m)
+                finish(m, t - 1)
 
             return carry
 
-        lax.fori_loop(0, 8, body, 0)
-        finish(7, m)
-        for t in (6, 7):
-            sent(t, m).wait_send()
-            saved(t, m).wait()
-        if m == 0:
+        return step
+
+    for i, (m, start) in enumerate(((0, 0), (0, 4), (1, 0))):
+        lax.fori_loop(start, start + 4, body(m, start), 0)
+        finish(m, start + 3)
+        free(m, start + 2)
+        free(m, start + 3)
+        if i == 0:
+            sc.near(2)
+            sc.near(0)
+            sc.along(3)
+        if i == 1:
             sc.along(1)
-        if m == 1:
             sc.along(2)
-            sc.along(3)
     sc.along(0)
     sc.end()
     stay.wait()
@@ -697,7 +749,7 @@
         hop(d).wait()
 
 
-def expert_weights(p1, rdm, xr, pg, hid, gg, ug, wout, n2g, tokens, att, cot, gain, cid):
+def expert_weights(p1, xr, pg, hid, gg, ug, wout, n2g, tokens, att, cot, gain, cid):
     _, rows, width = p1.shape
     n, ff = gg.shape
     seq = wout.shape[0]
@@ -712,18 +764,18 @@
             f(rows, width), b(width, ff), b(width, ff), b(ff, width), b(rows, width), f(rows, width), f(1, width),
             b(16 * rows, HD),
         ],
-        in_specs=[ANY] * 8 + [VM] * 5,
+        in_specs=[ANY] * 7 + [VM] * 5,
         out_specs=[VM] + [ANY] * 3 + [VM] * 3 + [ANY],
         scratch_shapes=[
-            v(16, rows, width), v(2, seq, 256), v(rows, width),
-            v(n, width), v(n, width), v(n, ff), v(n, ff), v(n, ff), v(2, r, w), v(2, r, w), v(3, 8, r, w),
+            v(16, rows, width), v(2, seq, HD), v(rows, width),
+            v(n, width), v(n, width), v(n, ff), v(n, ff), v(n, ff), v(2, 2, r, w), v(12, 2, r, w),
         ]
         + scatter_bufs(rows, width)
-        + [sem(7), sem(2), sem(2), sem(3, 8), sem(2), sem(16), sem(16), sem()]
+        + [sem(6), sem(2), sem(2), sem(12), sem(2, 2), sem(16), sem(16), sem()]
         + SCATTER_SEMS,
         compiler_params=params(cid, 63),
         name="expert_weights",
-    )(p1, rdm, xr, pg, hid, gg, ug, wout, n2g, tokens, att, cot, gain)
+    )(p1, xr, pg, hid, gg, ug, wout, n2g, tokens, att, cot, gain)
 
 
 def back_kernel(
@@ -752,18 +804,11 @@
     pair = push_pair(opart.at[:, pl.ds(other, hr)], opair, ops, opr)
     dkt[...] = jnp.zeros_like(dkt)
     dvt[...] = jnp.zeros_like(dvt)
-    so = Scatter(opair, osum, hr, (ord_, orx, ory, orz), sems[:8])
-    sn = Scatter(part, ngrad, HD, (rd, rx, ry, rz), sems[8:16])
-    pair.wait_recv()
-
+    so = PlainScatter(opair, osum, hr, (ord_, orx, ory, orz), sems[:10])
+    sn = PlainScatter(part, ngrad, HD, (rd, rx, ry, rz), sems[10:20])
     def out_pair(b, carry):
         opair[b] = (opair[b].astype(F32) + opart[b, pl.ds(mine, hr)].astype(F32)).astype(BF)
         return carry
-
-    lax.fori_loop(0, 16, out_pair, 0)
-    order = (1, 2, 3, 0)
-    for j in order:
-        so.far(j)
 
     def attend_rows(i, carry):
         row = blk(i)
@@ -782,11 +827,13 @@
 
     n = q.shape[0] // HD
     lax.fori_loop(0, n // 2, attend_rows, 0)
-    for j in order:
+    pair.wait_recv()
+    lax.fori_loop(0, 16, out_pair, 0)
+    for j in FAR_FIRST:
+        so.far(j)
+    lax.fori_loop(n // 2, n, attend_rows, 0)
+    for j in FAR_FIRST:
         so.near(j)
-    lax.fori_loop(n // 2, n, attend_rows, 0)
-    for j in order:
-        so.along(j)
 
     def turn_back(i, carry):
         row = blk(i)
@@ -806,9 +853,11 @@
         b = place_of(kk, j)
         part[b] = dot(pgrad[blk(b)], wh[...], 1, 0).astype(BF)
 
-    for kk in order:
+    for kk in FAR_FIRST:
         back_block(3, kk)
         sn.far(kk)
+    for j in FAR_FIRST:
+        so.along(j)
     for t, c in enumerate(tiles):
         if t + 1 < len(tiles):
             tiles[t + 1].start()
@@ -820,7 +869,7 @@
     keep = pltpu.make_async_copy(ostage, out_t.at[pl.ds(mine, hr)], lo)
     keep.start()
     give = push_pair(ostage, out_t.at[pl.ds(mine, hr)], ofs, ofr)
-    for kk in order:
+    for kk in FAR_FIRST:
         back_block(1, kk)
         back_block(2, kk)
         sn.near(kk)
@@ -839,9 +888,9 @@
         def _():
             pltpu.make_async_copy(qpair.at[s], dst, tr.at[slot]).start()
 
-    for kk in order:
+    for kk in FAR_FIRST:
         back_block(0, kk)
-    for kk in order:
+    for kk in FAR_FIRST:
         sn.along(kk)
     fc = []
     for s in range(3):
@@ -883,9 +932,9 @@
             vf(HD, seq), vf(HD, seq), vb(seq, 3 * HD), vb(3 * HD, seq),
             vb(16, rows, width), vb(16, rows // 2, width), vf(rows // 2, width), vb(rows // 2, width),
         ]
-        + scatter_bufs(rows // 2, width)
+        + plain_bufs(rows // 2, width)
         + [vb(16, rows, width)]
-        + scatter_bufs(rows, width)
+        + plain_bufs(rows, width)
         + [vb(2, seq, 256), vb(3 * HD, width), vb(3, HD // 2, width)]
         + [sem(), sem(), sem(), sem(), sem(), sem(2), sem(3), sem(3), sem(3), sem(3), sem(3), sem(3)]
         + SCATTER_SEMS * 2,
@@ -948,13 +997,13 @@
     normed_all, meta_all, w_head, q, k, v, lse, context, dense_out = front(
         tokens, gain1_row, meta, qkv_weight, out_weight, cos_table, sin_table, seg, sk, 0
     )
-    attended, n2g, mix_part, mix_far, xr, pg, hidden, gg, ug = expert(
+    attended, n2g, mix_part, xr, pg, hidden, gg, ug = expert(
         context, dense_out, tokens, gain2_row, cotangent, meta_all, capacity,
         gate_weight[0], up_weight[0], down_weight[0], 3,
     )
     flat = lambda a: a.reshape(-1, a.shape[2])
     mixture, gate_g, up_g, down_g, attended_grad, middle_grad, gain2, cgh = expert_weights(
-        mix_part, mix_far, flat(xr), flat(pg), flat(hidden), flat(gg), flat(ug), flat(dense_out),
+        mix_part, flat(xr), flat(pg), flat(hidden), flat(gg), flat(ug), flat(dense_out),
         n2g, tokens, attended, cotangent, gain2_row, 5,
     )
     layer = stream + attended + mixture

time: 743 us -> 690 us (0.929)
  Pallas kernels: 693 us -> 641 us
    pallas_call x1, Pallas kernels: 260 us -> 241 us  [expert(): pl.pallas_call(expert_kernel, out_shape=[jax.ShapeDtypeStruct((rows, widt...]
    pallas_call x1, Pallas kernels: 160 us -> 144 us  [back(): pl.pallas_call(back_kernel, out_shape=[jax.ShapeDtypeStruct((rows, width)...]
    pallas_call x1, Pallas kernels: 159 us -> 145 us  [front(): pl.pallas_call(front_kernel, out_shape=[b(16, rows, width), f(16, *meta.s...]
    pallas_call x1, Pallas kernels: 23.2 us -> 12.8 us  [total(): pl.pallas_call(total_kernel, out_shape=[jax.ShapeDtypeStruct(x.shape, F32...]
    pallas_call x1, Pallas kernels: 91 us -> 98.5 us  [expert_weights(): pl.pallas_call(weights_kernel, out_shape=[f(rows, width), b(width, ff), b...]
where the time goes in v1:
time: 690 us; the launch traced here: 680 us
  Pallas kernels  641 us (93%)
  other arithmetic  32.1 us (5%)
    pallas_call x1, Pallas kernels, expert(): pl.pallas_call(expert_kernel, out_shape=[jax.ShapeDtypeStruct((rows, widt...  241 us
    pallas_call x1, Pallas kernels, front(): pl.pallas_call(front_kernel, out_shape=[b(16, rows, width), f(16, *meta.s...  145 us
    pallas_call x1, Pallas kernels, back(): pl.pallas_call(back_kernel, out_shape=[jax.ShapeDtypeStruct((rows, width)...  144 us
    pallas_call x1, Pallas kernels, expert_weights(): pl.pallas_call(weights_kernel, out_shape=[f(rows, width), b(width, ff), b...  98.5 us

profile of v1, /device:TPU:5, one launch (start us, length us, event | category | flops | bytes accessed | tf_op | source)
XLA Modules:
  0.0 680.5 jit_solution(18419795751091133074)
XLA Ops:
  0.6 1.4 fusion.11
  2.0 1.4 convert_select_fusion
  3.4 1.3 convert_bitcast_fusion.seg
  4.7 0.7 convert_bitcast_fusion.1
  5.4 1.3 pad_maximum_fusion.m_ref
  6.7 145.2 %front.1 = (bf16[16,128,2048]{2,1,0:T(8,128)(2,1)}, f32[16,16,128]{2,1,0:T(8,128)}, bf16[384,2048]{1,0:T(8,128)(2,1)}, bf16[2048,128]{1,0:T(8,128)(2,1)}, bf16[2...) custom-call(bf16[128,2048]{1,0:T(8,128)(2,1)} %tok.5, ...), custom_call_target="tpu_custom_call" | custom-call | tf_op jit(solution)/shard_map/front/pallas_call | solution.py:419
  152.5 241.3 %expert.1 = (f32[128,2048]{1,0:T(8,128)}, f32[128,2048]{1,0:T(8,128)}, bf16[16,128,2048]{2,1,0:T(8,128)(2,1)}, bf16[4,320,2048]{2,1,0:T(8,128)(2,1)}, bf16[4,320...) custom-call(bf16[128,2048]{1,0:T(8,128)(2,1)} %get-tuple-element.39., ...), custom_call_target="tpu_custom_call" | custom-call | tf_op jit(solution)/shard_map/expert/pallas_call | solution.py:583
  393.8 98.5 %expert_weights.1 = (f32[128,2048]{1,0:T(8,128)}, bf16[2048,1024]{1,0:T(8,128)(2,1)}, bf16[2048,1024]{1,0:T(8,128)(2,1)}, bf16[1024,2048]{1,0:T(8,128)(2,1)}, bf...) custom-call(bf16[16,128,2048]{2,1,0:T(8,128)(2,1)} %get-tuple-element.43.p1, ...), custom_call_target="tpu_custom_call" | custom-call | tf_op jit(solution)/shard_map/expert_weights/pallas_call | solution.py:761
  492.3 0.0 copy-start
  492.3 0.0 copy-start.3
  492.4 0.0 copy-start.7
  492.4 143.6 %back.1 = (f32[128,2048]{1,0:T(8,128)}, bf16[128,2048]{1,0:T(8,128)(2,1)}, bf16[384,2048]{1,0:T(8,128)(2,1)}) custom-call(bf16[2048,128]{1,0:T(8,128)(2,1)} %get-tuple-element.52.cgh, bf16[2048,128]{1,0:T(8,128)(2,1)} %get-tuple-element.53.q, bf16[2048,128]{1,0:T(8,128)(2,1)} %get-tuple-element.54.k, bf16[2048,128]{1,0:T(8,128)(2,1)} %get-tuple-element.55.v, ...), custom_call_target="tpu_custom_call" | custom-call | tf_op jit(solution)/shard_map/back/pallas_call | solution.py:922
  636.0 0.0 copy-start.8
  636.0 0.0 copy-done
  636.0 0.0 copy-done.3
  636.0 2.6 multiply_reduce_fusion
  638.7 0.0 copy-done.7
  638.7 1.5 fusion.6
  640.2 1.4 convert_reduce_fusion
  642.2 0.0 copy-done.8
  642.2 2.0 concatenate.7
  644.3 12.8 %total.1 = (f32[40,128]{1,0:T(8,128)S(1)}, f32[40,128]{1,0:T(8,128)S(1)}) custom-call(f32[40,128]{1,0:T(8,128)S(1)} %bitcast.36), custom_call_target="tpu_custom_call" | custom-call | tf_op jit(solution)/shard_map/total/pallas_call | solution.py:966
  657.1 0.6 slice.25
  657.6 1.2 fusion.10
  658.8 0.6 reshape.86
  659.4 0.0 copy-start.1
  659.4 11.9 %bitcast_convert_fusion.1 = (f32[1,2048,1024]{2,1,0:T(8,128)}, f32[1,2048,1024]{2,1,0:T(8,128)}) fusion(bf16[2048,1024]{1,0:T(8,128)(2,1)} %get-tuple-element.64, bf16[2048,1024]{1,0:T(8,128)(2,1)} %get-tuple-element.63), kind=kLoop, calls=%fused_computation.1 | loop fusion | flops 4194304 | bytes 25165824 | tf_op jit(solution)/shard_map/broadcast_in_dim | solution.py:1038
  671.4 0.0 copy-done.1
  671.4 0.0 copy-start.4
  671.4 4.4 bitcast_convert_fusion
  675.8 0.0 copy-start.2
  675.8 0.0 copy-start.5
  675.8 0.0 copy-done.4
  675.8 0.0 copy-start.6
  675.8 2.0 convert_element_type.29
  677.9 0.0 copy-done.2
  677.9 0.1 copy-done.5
  677.9 1.3 fusion.4
  679.2 0.0 copy-done.6
  679.2 1.1 convert_element_type.30
  (3 shorter events, 0.0 us)
Async XLA Ops:
  492.3 143.7 %copy-start = (bf16[128,2048]{1,0:T(8,128)(2,1)S(1)}, bf16[128,2048]{1,0:T(8,128)(2,1)}, u32[]{:S(2)}) copy-start(bf16[128,2048]{1,0:T(8,128)(2,1)} %tok.5) | copy-start | bytes 1572868
  492.3 143.7 %copy-start.3 = (f32[128,2048]{1,0:T(8,128)S(1)}, f32[128,2048]{1,0:T(8,128)}, u32[]{:S(2)}) copy-start(f32[128,2048]{1,0:T(8,128)} %get-tuple-element.42.att) | copy-start | bytes 3145732
  492.4 146.3 %copy-start.7 = (f32[1,2048]{1,0:T(1,128)S(1)}, f32[1,2048]{1,0:T(1,128)}, u32[]{:S(2)}) copy-start(f32[1,2048]{1,0:T(1,128)} %get-tuple-element.81.gain) | copy-start | bytes 24580
  636.0 6.2 copy-start.8
  659.4 11.9 %copy-start.1 = (bf16[1024,2048]{1,0:T(8,128)(2,1)S(1)}, bf16[1024,2048]{1,0:T(8,128)(2,1)}, u32[]{:S(2)}) copy-start(bf16[1024,2048]{1,0:T(8,128)(2,1)} %get-tuple-element.65) | copy-start | bytes 12582916
  671.4 4.5 copy-start.4
  675.8 2.0 copy-start.2
  675.8 2.1 copy-start.5
  675.8 3.4 copy-start.6

commit v2 on v1

--- a/solution.py
+++ b/solution.py
@@ -158,6 +158,7 @@
 class Scatter:
     def __init__(self, part, out, rows, bufs, sems):
         self.part, self.out, self.half, self.bufs, self.sems, self.p = part, out, rows // 2, bufs, sems, places()
+        self.at = self.p
         self.da, self.db, self.xc, self.yc, self.zc, self.vc = {}, {}, {}, {}, {}, {}
 
     def lift(self, k):
@@ -215,7 +216,7 @@
     def far(self, k):
         ds, dr = self.sems[:2]
         rd, h, p = self.bufs[0], self.half, self.p
-        b = p["D"][k]
+        b = self.at["D"][k]
         self.da[k] = push(self.part.at[b, pl.ds(0, h)], rd.at[2 * k], ds.at[k, 0], dr.at[k, 0], p["Y"][0])
         self.db[k] = push(self.part.at[b, pl.ds(h, h)], rd.at[2 * k + 1], ds.at[k, 1], dr.at[k, 1], p["X"][0])
 
@@ -223,14 +224,27 @@
         xs, xr, ys, yr = self.sems[2:6]
         rd, rx, ry = self.bufs[:3]
         part, h, p = self.part, self.half, self.p
-        b = p["X"][k]
+        b = self.at["X"][k]
         self.da[k].wait_recv()
         part[b, pl.ds(0, h)] = (part[b, pl.ds(0, h)].astype(F32) + rd[2 * k].astype(F32)).astype(BF)
         self.xc[k] = push(part.at[b], rx.at[k], xs.at[k], xr.at[k], p["X"][0])
-        b = p["Y"][k]
+        b = self.at["Y"][k]
         self.db[k].wait_recv()
         part[b, pl.ds(h, h)] = (part[b, pl.ds(h, h)].astype(F32) + rd[2 * k + 1].astype(F32)).astype(BF)
         self.yc[k] = push(part.at[b], ry.at[k], ys.at[k], yr.at[k], p["Y"][0])
+
+    def along(self, k):
+        zs, zr = self.sems[6:8]
+        rx, ry, rz = self.bufs[1:4]
+        part, b = self.part, self.at["col"][k]
+        self.xc[k].wait_recv()
+        self.yc[k].wait_recv()
+        total = part[b].astype(F32) + rx[k].astype(F32) + ry[k].astype(F32)
+        if k:
+            part[b] = total.astype(BF)
+            self.zc[k] = push(part.at[b], rz.at[k], zs.at[k], zr.at[k], self.p["col"][k])
+        else:
+            self.out[...] = total
 
 
 def plain_bufs(rows, width):
@@ -316,21 +330,24 @@
     g.over(0)
     g.far(2)
     g.near(3)
+    go.begin()
+    g.over(2)
     pc = []
     for s in range(3):
         dst = wh.at[half(s, core)]
         pltpu.make_async_copy(dst, dst, wr.at[s]).wait()
         pc.append(push_pair(dst, dst, ps.at[s], pr.at[s]))
-    go.begin()
+    go.near(1)
     for p in pc:
         p.wait_recv()
     g.ready(0)
     project_plane(0)
     g.ready(1)
     project_plane(1)
-    g.over(2)
     g.ready(2)
     project_plane(2)
+    go.far(0)
+    go.near(2)
     g.ready(3)
     project_plane(3)
     saves = [pltpu.make_async_copy(nall, nall_o, no), pltpu.make_async_copy(wh, wh_o, wo)]
@@ -362,14 +379,6 @@
         hop(d).start()
         return carry
 
-    lax.fori_loop(1, 8, attend_send, 0)
-    go.near(1)
-    go.far(0)
-    go.near(2)
-    lax.fori_loop(8, 16, attend_send, 0)
-    attend_rows(0, 0)
-    stay = pltpu.make_async_copy(ctxh.at[blk(me)], ctx.at[:, blk(me)], co)
-    stay.start()
     oc = []
 
     def swap_plane(c):
@@ -378,11 +387,17 @@
         here = oall.at[pl.ds(4 * z, 4), pl.ds(pl.multiple_of(core * hr, hr), hr)]
         oc.append(push_pair(here, here, os_.at[c], or_.at[c]))
 
+    lax.fori_loop(1, 6, attend_send, 0)
     go.over(0)
     go.far(2)
     go.near(3)
+    lax.fori_loop(6, 12, attend_send, 0)
     swap_plane(0)
     swap_plane(1)
+    lax.fori_loop(12, 16, attend_send, 0)
+    attend_rows(0, 0)
+    stay = pltpu.make_async_copy(ctxh.at[blk(me)], ctx.at[:, blk(me)], co)
+    stay.start()
     go.over(2)
     swap_plane(2)
     swap_plane(3)
@@ -781,7 +796,7 @@
 def back_kernel(
     cgh, q, k, v, seg, sk, lse, cosf, sinf, wh, nall, ag, ctx,
     ngrad, out_t, qkv_t,
-    dkt, dvt, pgrad, pgt, opart, opair, osum, ostage, ord_, orx, ory, orz,
+    dkt, dvt, pgrad, pgt, opair, osum, ostage, ord_, orx, ory, orz,
     part, rd, rx, ry, rz, ntile, qpart, qpair,
     lo, ops, opr, ofs, ofr, nsem, qs, qr, ts, tr, fs, fr, *sems,
 ):
@@ -796,19 +811,25 @@
         for t in range(wh.shape[1] // 256)
     ]
 
-    def out_block(b, carry):
-        opart[b] = dot(ag[:, blk(b)], ctx[...], 0, 0).astype(BF)
-        return carry
-
-    lax.fori_loop(0, 16, out_block, 0)
-    pair = push_pair(opart.at[:, pl.ds(other, hr)], opair, ops, opr)
+    pairs = {}
+    for j in (3, 1, 2, 0):
+        for kk in range(4):
+            part[4 * j + kk] = dot(ag[:, blk(place_of(kk, j))], ctx[...], 0, 0).astype(BF)
+        group = pl.ds(4 * j, 4)
+        pairs[j] = push_pair(part.at[group, pl.ds(other, hr)], opair.at[group], ops.at[j], opr.at[j])
     dkt[...] = jnp.zeros_like(dkt)
     dvt[...] = jnp.zeros_like(dvt)
     so = PlainScatter(opair, osum, hr, (ord_, orx, ory, orz), sems[:10])
+    so.at = {name: [4 * j + kk for kk in range(4)] for j, name in enumerate(("col", "X", "Y", "D"))}
     sn = PlainScatter(part, ngrad, HD, (rd, rx, ry, rz), sems[10:20])
-    def out_pair(b, carry):
-        opair[b] = (opair[b].astype(F32) + opart[b, pl.ds(mine, hr)].astype(F32)).astype(BF)
-        return carry
+    def out_pair(j):
+        pairs[j].wait_recv()
+
+        def add(b, carry):
+            opair[b] = (opair[b].astype(F32) + part[b, pl.ds(mine, hr)].astype(F32)).astype(BF)
+            return carry
+
+        lax.fori_loop(4 * j, 4 * j + 4, add, 0)
 
     def attend_rows(i, carry):
         row = blk(i)
@@ -826,14 +847,23 @@
         return carry
 
     n = q.shape[0] // HD
-    lax.fori_loop(0, n // 2, attend_rows, 0)
-    pair.wait_recv()
-    lax.fori_loop(0, 16, out_pair, 0)
+    q4 = n // 4
+    lax.fori_loop(0, q4 // 2, attend_rows, 0)
+    out_pair(3)
     for j in FAR_FIRST:
         so.far(j)
-    lax.fori_loop(n // 2, n, attend_rows, 0)
-    for j in FAR_FIRST:
-        so.near(j)
+    lax.fori_loop(q4 // 2, 2 * q4, attend_rows, 0)
+    out_pair(1)
+    out_pair(2)
+    so.near(3)
+    so.near(2)
+    lax.fori_loop(2 * q4, 3 * q4, attend_rows, 0)
+    so.near(1)
+    so.near(0)
+    out_pair(0)
+    lax.fori_loop(3 * q4, n, attend_rows, 0)
+    for c in pairs.values():
+        c.wait_send()
 
     def turn_back(i, carry):
         row = blk(i)
@@ -906,7 +936,6 @@
 
     keep.wait()
     give.wait()
-    pair.wait_send()
     for c in qc:
         c.wait_send()
     for c in fc:
@@ -930,13 +959,13 @@
         out_specs=[VM, ANY, ANY],
         scratch_shapes=[
             vf(HD, seq), vf(HD, seq), vb(seq, 3 * HD), vb(3 * HD, seq),
-            vb(16, rows, width), vb(16, rows // 2, width), vf(rows // 2, width), vb(rows // 2, width),
+            vb(16, rows // 2, width), vf(rows // 2, width), vb(rows // 2, width),
         ]
         + plain_bufs(rows // 2, width)
         + [vb(16, rows, width)]
         + plain_bufs(rows, width)
         + [vb(2, seq, 256), vb(3 * HD, width), vb(3, HD // 2, width)]
-        + [sem(), sem(), sem(), sem(), sem(), sem(2), sem(3), sem(3), sem(3), sem(3), sem(3), sem(3)]
+        + [sem(), sem(4), sem(4), sem(), sem(), sem(2), sem(3), sem(3), sem(3), sem(3), sem(3), sem(3)]
         + SCATTER_SEMS * 2,
         compiler_params=params(cid, 62),
         name="back",

time: 690 us -> 667 us (0.967)
  Pallas kernels: 641 us -> 619 us
    pallas_call x1, Pallas kernels: 145 us -> 133 us  [front(): pl.pallas_call(front_kernel, out_shape=[b(16, rows, width), f(16, *meta.s...]
    pallas_call x1, Pallas kernels: 144 us -> 134 us  [back(): pl.pallas_call(back_kernel, out_shape=[jax.ShapeDtypeStruct((rows, width)...]
where the time goes in v2:
time: 667 us; the launch traced here: 658 us
  Pallas kernels  619 us (93%)
  other arithmetic  32.1 us (5%)
    pallas_call x1, Pallas kernels, expert(): pl.pallas_call(expert_kernel, out_shape=[jax.ShapeDtypeStruct((rows, widt...  240 us
    pallas_call x1, Pallas kernels, back(): pl.pallas_call(back_kernel, out_shape=[jax.ShapeDtypeStruct((rows, width)...  134 us
    pallas_call x1, Pallas kernels, front(): pl.pallas_call(front_kernel, out_shape=[b(16, rows, width), f(16, *meta.s...  133 us
    pallas_call x1, Pallas kernels, expert_weights(): pl.pallas_call(weights_kernel, out_shape=[f(rows, width), b(width, ff), b...  98.6 us

profile of v2, /device:TPU:5, one launch (start us, length us, event | category | flops | bytes accessed | tf_op | source)
XLA Modules:
  0.0 658.3 jit_solution(11333123440361080229)
XLA Ops:
  0.6 1.4 fusion.11
  2.0 1.4 convert_select_fusion
  3.4 1.3 convert_bitcast_fusion.seg
  4.7 0.7 convert_bitcast_fusion.1
  5.4 1.3 pad_maximum_fusion.m_ref
  6.7 133.4 %front.1 = (bf16[16,128,2048]{2,1,0:T(8,128)(2,1)}, f32[16,16,128]{2,1,0:T(8,128)}, bf16[384,2048]{1,0:T(8,128)(2,1)}, bf16[2048,128]{1,0:T(8,128)(2,1)}, bf16[2...) custom-call(bf16[128,2048]{1,0:T(8,128)(2,1)} %tok.5, ...), custom_call_target="tpu_custom_call" | custom-call | tf_op jit(solution)/shard_map/front/pallas_call | solution.py:434
  140.8 240.4 %expert.1 = (f32[128,2048]{1,0:T(8,128)}, f32[128,2048]{1,0:T(8,128)}, bf16[16,128,2048]{2,1,0:T(8,128)(2,1)}, bf16[4,320,2048]{2,1,0:T(8,128)(2,1)}, bf16[4,320...) custom-call(bf16[128,2048]{1,0:T(8,128)(2,1)} %get-tuple-element.39., ...), custom_call_target="tpu_custom_call" | custom-call | tf_op jit(solution)/shard_map/expert/pallas_call | solution.py:598
  381.2 98.6 %expert_weights.1 = (f32[128,2048]{1,0:T(8,128)}, bf16[2048,1024]{1,0:T(8,128)(2,1)}, bf16[2048,1024]{1,0:T(8,128)(2,1)}, bf16[1024,2048]{1,0:T(8,128)(2,1)}, bf...) custom-call(bf16[16,128,2048]{2,1,0:T(8,128)(2,1)} %get-tuple-element.43.p1, ...), custom_call_target="tpu_custom_call" | custom-call | tf_op jit(solution)/shard_map/expert_weights/pallas_call | solution.py:776
  479.8 0.0 copy-start
  479.8 0.0 copy-start.3
  479.8 0.0 copy-start.7
  479.8 134.0 %back.1 = (f32[128,2048]{1,0:T(8,128)}, bf16[128,2048]{1,0:T(8,128)(2,1)}, bf16[384,2048]{1,0:T(8,128)(2,1)}) custom-call(bf16[2048,128]{1,0:T(8,128)(2,1)} %get-tuple-element.52.cgh, bf16[2048,128]{1,0:T(8,128)(2,1)} %get-tuple-element.53.q, bf16[2048,128]{1,0:T(8,128)(2,1)} %get-tuple-element.54.k, bf16[2048,128]{1,0:T(8,128)(2,1)} %get-tuple-element.55.v, ...), custom_call_target="tpu_custom_call" | custom-call | tf_op jit(solution)/shard_map/back/pallas_call | solution.py:951
  613.8 0.0 copy-start.8
  613.8 0.0 copy-done
  613.8 0.0 copy-done.3
  613.8 2.6 multiply_reduce_fusion
  616.5 0.0 copy-done.7
  616.5 1.5 fusion.6
  618.0 1.4 convert_reduce_fusion
  620.0 0.0 copy-done.8
  620.0 2.0 concatenate.7
  622.1 12.8 %total.1 = (f32[40,128]{1,0:T(8,128)S(1)}, f32[40,128]{1,0:T(8,128)S(1)}) custom-call(f32[40,128]{1,0:T(8,128)S(1)} %bitcast.36), custom_call_target="tpu_custom_call" | custom-call | tf_op jit(solution)/shard_map/total/pallas_call | solution.py:995
  634.9 0.6 slice.25
  635.5 1.2 fusion.10
  636.6 0.6 reshape.86
  637.3 0.0 copy-start.1
  637.3 11.9 %bitcast_convert_fusion.1 = (f32[1,2048,1024]{2,1,0:T(8,128)}, f32[1,2048,1024]{2,1,0:T(8,128)}) fusion(bf16[2048,1024]{1,0:T(8,128)(2,1)} %get-tuple-element.64, bf16[2048,1024]{1,0:T(8,128)(2,1)} %get-tuple-element.63), kind=kLoop, calls=%fused_computation.1 | loop fusion | flops 4194304 | bytes 25165824 | tf_op jit(solution)/shard_map/broadcast_in_dim | solution.py:1067
  649.2 0.0 copy-done.1
  649.2 0.0 copy-start.4
  649.2 4.4 bitcast_convert_fusion
  653.6 0.0 copy-start.2
  653.6 0.0 copy-start.5
  653.6 0.0 copy-done.4
  653.6 0.0 copy-start.6
  653.6 2.0 convert_element_type.29
  655.7 0.0 copy-done.2
  655.7 0.1 copy-done.5
  655.7 1.3 fusion.4
  657.0 0.0 copy-done.6
  657.0 1.1 convert_element_type.30
  (3 shorter events, 0.0 us)
Async XLA Ops:
  479.8 134.0 %copy-start = (bf16[128,2048]{1,0:T(8,128)(2,1)S(1)}, bf16[128,2048]{1,0:T(8,128)(2,1)}, u32[]{:S(2)}) copy-start(bf16[128,2048]{1,0:T(8,128)(2,1)} %tok.5) | copy-start | bytes 1572868
  479.8 134.0 %copy-start.3 = (f32[128,2048]{1,0:T(8,128)S(1)}, f32[128,2048]{1,0:T(8,128)}, u32[]{:S(2)}) copy-start(f32[128,2048]{1,0:T(8,128)} %get-tuple-element.42.att) | copy-start | bytes 3145732
  479.8 136.7 %copy-start.7 = (f32[1,2048]{1,0:T(1,128)S(1)}, f32[1,2048]{1,0:T(1,128)}, u32[]{:S(2)}) copy-start(f32[1,2048]{1,0:T(1,128)} %get-tuple-element.81.gain) | copy-start | bytes 24580
  613.8 6.2 copy-start.8
  637.3 11.9 %copy-start.1 = (bf16[1024,2048]{1,0:T(8,128)(2,1)S(1)}, bf16[1024,2048]{1,0:T(8,128)(2,1)}, u32[]{:S(2)}) copy-start(bf16[1024,2048]{1,0:T(8,128)(2,1)} %get-tuple-element.65) | copy-start | bytes 12582916
  649.2 4.5 copy-start.4
  653.6 2.0 copy-start.2
  653.6 2.1 copy-start.5
  653.6 3.4 copy-start.6

commit v3 on v2

--- a/solution.py
+++ b/solution.py
@@ -795,7 +795,10 @@
 
 def back_kernel(
     cgh, q, k, v, seg, sk, lse, cosf, sinf, wh, nall, ag, ctx,
-    ngrad, out_t, qkv_t,
+    tok, att, mix, mg, gain1, gain2,
+    layer_o, tok_g, stat_o, gain_o, out_t, qkv_t,
+    ngrad, valid, gsum, early, late, early_got, late_got, both, both_got,
+    es, er, hs, hr_, bs, br,
     dkt, dvt, pgrad, pgt, opair, osum, ostage, ord_, orx, ory, orz,
     part, rd, rx, ry, rz, ntile, qpart, qpair,
     lo, ops, opr, ofs, ofr, nsem, qs, qr, ts, tr, fs, fr, *sems,
@@ -817,6 +820,26 @@
             part[4 * j + kk] = dot(ag[:, blk(place_of(kk, j))], ctx[...], 0, 0).astype(BF)
         group = pl.ds(4 * j, 4)
         pairs[j] = push_pair(part.at[group, pl.ds(other, hr)], opair.at[group], ops.at[j], opr.at[j])
+    strips = [slice(e * HD, (e + 1) * HD) for e in range(16)]
+    valid[...] = (column(seg, me) != 0.0).astype(F32)
+    early[...] = jnp.zeros_like(early)
+    for e, cut in enumerate(strips):
+        early[e : e + 1, :] = gain2[:, cut]
+    early[19:20, :] = jnp.broadcast_to(jnp.sum(valid[...], 0, keepdims=True) * 16.0, (1, HD))
+
+    def layer_rows(i, carry):
+        rows = pl.ds(pl.multiple_of(i * 16, 16), 16)
+        layer = tok[rows].astype(F32) + att[rows] + mix[rows]
+        layer_o[rows] = layer.astype(BF)
+        for e, field in enumerate((layer, att[rows], mix[rows])):
+            square = field * field * valid[rows]
+            early[16 + e : 17 + e, :] += jnp.sum(sum(square[:, cut] for cut in strips), 0, keepdims=True)
+        return carry
+
+    lax.fori_loop(0, HD // 16, layer_rows, 0)
+    others = [lax.rem(me + d, 16) for d in range(1, 16)]
+    sends = [push(early, early_got.at[me], es.at[d + 1], er.at[d + 1], to) for d, to in enumerate(others)]
+    early_got[me] = early[...]
     dkt[...] = jnp.zeros_like(dkt)
     dvt[...] = jnp.zeros_like(dvt)
     so = PlainScatter(opair, osum, hr, (ord_, orx, ory, orz), sems[:10])
@@ -934,6 +957,38 @@
         def _():
             pltpu.make_async_copy(qpair.at[s], qpair.at[s], ts.at[s]).wait()
 
+    gsum[...] = jnp.zeros_like(gsum)
+
+    def norm_rows(i, carry):
+        rows = pl.ds(pl.multiple_of(i * 16, 16), 16)
+        pull, gains = rmsnorm_pull(tok[rows].astype(F32), gain1[...], ngrad[rows])
+        tok_g[rows] = mg[rows] + pull
+        gsum[...] += jnp.sum(gains, 0, keepdims=True)
+        return carry
+
+    lax.fori_loop(0, HD // 16, norm_rows, 0)
+    for e, cut in enumerate(strips):
+        late[e : e + 1, :] = gsum[:, cut]
+    sends += [push(late, late_got.at[me], hs.at[d + 1], hr_.at[d + 1], to) for d, to in enumerate(others)]
+    late_got[me] = late[...]
+    for c in sends:
+        c.wait_recv()
+
+    def over_devices(got):
+        total = got[0]
+        for e in range(1, 16):
+            total = total + got[e]
+        return total
+
+    both[:16, :] = over_devices(late_got)
+    first = over_devices(early_got)
+    both[16:, :] = first[:16]
+    stat_o[...] = first[16:]
+    across = push_pair(both, both_got, bs, br)
+    across.wait()
+    gain_o[...] = both[...] + both_got[...]
+    for c in sends:
+        c.wait_send()
     keep.wait()
     give.wait()
     for c in qc:
@@ -942,7 +997,7 @@
         c.wait()
 
 
-def back(cgh, q, k, v, seg, sk, lse, cosf, sinf, wh, nall, ag, ctx, cid):
+def back(cgh, q, k, v, seg, sk, lse, cosf, sinf, wh, nall, ag, ctx, tok, att, mix, mg, gain1, gain2, cid):
     rows, width = ag.shape
     seq = q.shape[0]
     vb = lambda *shape: pltpu.VMEM(shape, BF)
@@ -951,13 +1006,18 @@
     return pl.pallas_call(
         back_kernel,
         out_shape=[
+            jax.ShapeDtypeStruct((rows, width), BF),
             jax.ShapeDtypeStruct((rows, width), F32),
+            jax.ShapeDtypeStruct((8, HD), F32),
+            jax.ShapeDtypeStruct((32, HD), F32),
             jax.ShapeDtypeStruct((rows, width), BF),
             jax.ShapeDtypeStruct((3 * HD, width), BF),
         ],
-        in_specs=[VM] * 10 + [ANY, VM, VM],
-        out_specs=[VM, ANY, ANY],
+        in_specs=[VM] * 10 + [ANY] + [VM] * 8,
+        out_specs=[VM] * 4 + [ANY, ANY],
         scratch_shapes=[
+            vf(rows, width), vf(rows, 1), vf(1, width), vf(24, HD), vf(16, HD), vf(16, 24, HD), vf(16, 16, HD),
+            vf(32, HD), vf(32, HD), sem(16), sem(16), sem(16), sem(16), sem(), sem(),
             vf(HD, seq), vf(HD, seq), vb(seq, 3 * HD), vb(3 * HD, seq),
             vb(16, rows // 2, width), vf(rows // 2, width), vb(rows // 2, width),
         ]
@@ -969,38 +1029,7 @@
         + SCATTER_SEMS * 2,
         compiler_params=params(cid, 62),
         name="back",
-    )(cgh, q, k, v, seg, sk, lse, cosf, sinf, wh, nall, ag, ctx)
-
-
-def total_kernel(x, dp_o, pair_o, got, fromp, ss, rs, ps, pr):
-    me = lax.axis_index("dp")
-    barrier([lax.rem(me + d, 16) for d in range(1, 16)], pair=True)
-    sent = [push(x, got.at[me], ss.at[d], rs.at[d], lax.rem(me + d, 16)) for d in range(1, 16)]
-    got[me] = x[...]
-    for c in sent:
-        c.wait_recv()
-    acc = got[0]
-    for j in range(1, 16):
-        acc = acc + got[j]
-    dp_o[...] = acc
-    c = push_pair(dp_o, fromp, ps, pr)
-    c.wait()
-    pair_o[...] = acc + fromp[...]
-    for c in sent:
-        c.wait_send()
-
-
-def total(x, cid):
-    sem = pltpu.SemaphoreType.DMA
-    return pl.pallas_call(
-        total_kernel,
-        out_shape=[jax.ShapeDtypeStruct(x.shape, F32)] * 2,
-        in_specs=[VM],
-        out_specs=[VM, VM],
-        scratch_shapes=[pltpu.VMEM((16,) + x.shape, F32), pltpu.VMEM(x.shape, F32), sem((16,)), sem((16,)), sem, sem],
-        compiler_params=params(cid, 16),
-        name="total",
-    )(x)
+    )(cgh, q, k, v, seg, sk, lse, cosf, sinf, wh, nall, ag, ctx, tok, att, mix, mg, gain1, gain2)
 
 
 def rotary_tables(length):
@@ -1016,9 +1045,7 @@
 ):
     rows, width = tokens.shape
     seq = segments.shape[0]
-    me = lax.axis_index("dp")
     gain1_row, gain2_row = norm_gain[:1], norm_gain[1:]
-    stream = tokens.astype(F32)
     meta = jnp.concatenate([routes.astype(F32).T, route_weight.T], 0)
     seg = segments.astype(F32).reshape(16, rows)
     sk = jnp.where(segments == 0, -1.0, segments.astype(F32))[None, :]
@@ -1035,31 +1062,17 @@
         mix_part, flat(xr), flat(pg), flat(hidden), flat(gg), flat(ug), flat(dense_out),
         n2g, tokens, attended, cotangent, gain2_row, 5,
     )
-    layer = stream + attended + mixture
-    own_seg = lax.dynamic_slice_in_dim(segments, me * rows, rows)
-    valid = (own_seg != 0).astype(F32)
-    sums = jnp.stack(
-        [
-            jnp.sum(valid * jnp.sum(layer * layer, -1)),
-            jnp.sum(valid * jnp.sum(attended * attended, -1)),
-            jnp.sum(valid * jnp.sum(mixture * mixture, -1)),
-            jnp.sum(valid) * width,
-        ]
+    layer_out, tokens_grad, stat_lanes, gain_pair, out_total, qkv_total = back(
+        cgh, q, k, v, seg, sk, lse, cos_table, sin_table, w_head, flat(normed_all), attended_grad, context,
+        tokens, attended, mixture, middle_grad, gain1_row, gain2, 6,
     )
-    normed_grad, out_total, qkv_total = back(
-        cgh, q, k, v, seg, sk, lse, cos_table, sin_table, w_head, flat(normed_all), attended_grad, context, 6
-    )
-    sg, gain1 = rmsnorm_pull(stream, gain1_row, normed_grad)
-    tokens_grad = middle_grad + sg
-    small = jnp.concatenate([jnp.sum(gain1, 0), gain2[0], sums, jnp.zeros((1024 - sums.size,), F32)]).reshape(-1, HD)
-    in_group, in_pair = total(small, 4)
-    seq_sums = in_group.reshape(-1)[2 * width : 2 * width + 4]
-    gain_pair = in_pair.reshape(-1)[: 2 * width].reshape(2, width)
+    seq_sums = jnp.sum(stat_lanes, 1)
+    gain_pair = gain_pair.reshape(2, width)
     stat_row = jnp.sqrt(seq_sums[:3] / seq_sums[3]).reshape(1, 3)
     groups = lax.axis_size("grp")
     over = lambda a: a.astype(F32) if groups == 2 else lax.psum(a.astype(BF), "grp").astype(F32) * 0.5
     return (
-        layer.astype(BF),
+        layer_out,
         tokens_grad,
         over(qkv_total),
         over(out_total),

time: 667 us -> 664 us (level)
    pallas_call x1, Pallas kernels: 134 us -> 147 us  [back(): pl.pallas_call(back_kernel, out_shape=[jax.ShapeDtypeStruct((rows, width)...]
    pallas_call x1 -> x0, Pallas kernels: 12.8 us -> none  [total(): pl.pallas_call(total_kernel, out_shape=[jax.ShapeDtypeStruct(x.shape, F32...]
where the time goes in v3:
time: 664 us; the launch traced here: 654 us
  Pallas kernels  619 us (93%)
  other arithmetic  27.4 us (4%)
    pallas_call x1, Pallas kernels, expert(): pl.pallas_call(expert_kernel, out_shape=[jax.ShapeDtypeStruct((rows, widt...  241 us
    pallas_call x1, Pallas kernels, back(): pl.pallas_call(back_kernel, out_shape=[jax.ShapeDtypeStruct((rows, width)...  147 us
    pallas_call x1, Pallas kernels, front(): pl.pallas_call(front_kernel, out_shape=[b(16, rows, width), f(16, *meta.s...  133 us
    pallas_call x1, Pallas kernels, expert_weights(): pl.pallas_call(weights_kernel, out_shape=[f(rows, width), b(width, ff), b...  98.4 us

profile of v3, /device:TPU:5, one launch (start us, length us, event | category | flops | bytes accessed | tf_op | source)
XLA Modules:
  0.0 653.5 jit_solution(9853746839884462381)
XLA Ops:
  1.3 0.7 convert_bitcast_fusion.1
  2.0 1.3 pad_maximum_fusion.m_ref
  3.3 1.3 convert_bitcast_fusion.seg
  4.6 1.4 convert_select_fusion
  5.9 1.4 fusion
  7.3 133.4 %front.1 = (bf16[16,128,2048]{2,1,0:T(8,128)(2,1)}, f32[16,16,128]{2,1,0:T(8,128)}, bf16[384,2048]{1,0:T(8,128)(2,1)}, bf16[2048,128]{1,0:T(8,128)(2,1)}, bf16[2...) custom-call(bf16[128,2048]{1,0:T(8,128)(2,1)} %tok.7, ...), custom_call_target="tpu_custom_call" | custom-call | tf_op jit(solution)/shard_map/front/pallas_call | solution.py:434
  140.7 240.5 %expert.1 = (f32[128,2048]{1,0:T(8,128)}, f32[128,2048]{1,0:T(8,128)}, bf16[16,128,2048]{2,1,0:T(8,128)(2,1)}, bf16[4,320,2048]{2,1,0:T(8,128)(2,1)}, bf16[4,320...) custom-call(bf16[128,2048]{1,0:T(8,128)(2,1)} %get-tuple-element.40., ...), custom_call_target="tpu_custom_call" | custom-call | tf_op jit(solution)/shard_map/expert/pallas_call | solution.py:598
  381.3 98.4 %expert_weights.1 = (f32[128,2048]{1,0:T(8,128)}, bf16[2048,1024]{1,0:T(8,128)(2,1)}, bf16[2048,1024]{1,0:T(8,128)(2,1)}, bf16[1024,2048]{1,0:T(8,128)(2,1)}, bf...) custom-call(bf16[16,128,2048]{2,1,0:T(8,128)(2,1)} %get-tuple-element.43.p1, ...), custom_call_target="tpu_custom_call" | custom-call | tf_op jit(solution)/shard_map/expert_weights/pallas_call | solution.py:776
  479.7 147.0 %back.1 = (bf16[128,2048]{1,0:T(8,128)(2,1)}, f32[128,2048]{1,0:T(8,128)}, f32[8,128]{1,0:T(8,128)}, f32[32,128]{1,0:T(8,128)}, bf16[128,2048]{1,0:T(8,128)(2,1)}, /*index=5*/bf16[384,2048]{1,0:T(8,128)(2,1)}) custom-call(bf16[2048,128]{1,0:T(8,128)(2,1)} %get-tuple-element.51.cgh, bf16[2048,128]{1,0:T(8,128)(2,1)} %get-tuple-element.52.q, ...), custom_call_target="tpu_custom_call" | custom-call | tf_op jit(solution)/shard_map/back/pallas_call | solution.py:1006
  626.7 0.8 reduce_sum.9
  627.5 0.6 slice.15
  628.1 1.2 sqrt_bitcast_fusion
  629.2 1.3 reshape.56
  630.6 0.0 copy-start
  630.6 2.3 convert_element_type.19
  632.8 3.4 convert_element_type.18
  636.3 0.0 copy-done
  636.3 0.0 copy-start.1
  636.3 4.4 bitcast_convert_fusion
  640.7 0.0 copy-done.1
  640.7 0.0 copy-start.3
  640.7 0.0 copy-start.2
  640.8 10.6 %bitcast_convert_fusion.1 = (f32[1,2048,1024]{2,1,0:T(8,128)}, f32[1,2048,1024]{2,1,0:T(8,128)}) fusion(bf16[2048,1024]{1,0:T(8,128)(2,1)} %get-tuple-element.67, bf16[2048,1024]{1,0:T(8,128)(2,1)S(1)} %copy-done.1), kind=kLoop, calls=%fused_computation.1 | loop fusion | flops 4194304 | bytes 25165824 | tf_op jit(solution)/shard_map/broadcast_in_dim | solution.py:1080
  651.3 0.0 copy-done.3
  651.3 0.8 copy.26
  652.1 0.0 copy-done.2
  652.1 1.0 copy.27
Async XLA Ops:
  630.6 5.7 copy-start
  636.3 4.5 copy-start.1
  640.7 10.6 %copy-start.3 = (bf16[128,2048]{1,0:T(8,128)(2,1)S(1)}, bf16[128,2048]{1,0:T(8,128)(2,1)}, u32[]{:S(2)}) copy-start(bf16[128,2048]{1,0:T(8,128)(2,1)} %get-tuple-element.84) | copy-start | bytes 1572868
  640.7 11.4 %copy-start.2 = (f32[128,2048]{1,0:T(8,128)S(1)}, f32[128,2048]{1,0:T(8,128)}, u32[]{:S(2)}) copy-start(f32[128,2048]{1,0:T(8,128)} %get-tuple-element.85) | copy-start | bytes 3145732

commit v4 on v3

--- a/solution.py
+++ b/solution.py
@@ -95,7 +95,7 @@
         self.mine.start()
         self.xc = {0: push(src, self.block(me), xs.at[0], xr.at[0], p["X"][0])}
         self.yc = {0: push(src, self.block(me), ys.at[0], yr.at[0], p["Y"][0])}
-        self.zc = {k: push(src, self.block(me), zs.at[k], zr.at[k], p["col"][k]) for k in (1, 2, 3)}
+        self.zc = {k: push(src, self.block(me), zs.at[k], zr.at[k], p["col"][k]) for k in (1, 2)}
         self.dc, self.vc = {}, {}
 
     def near(self, k):
@@ -103,6 +103,9 @@
         p = self.p
         self.zc[k].wait_recv()
         b = self.block(p["col"][k])
+        if k == 2:
+            zs, zr = self.sems[:2]
+            self.zc[3] = push(b, b, zs.at[3], zr.at[3], p["col"][1])
         self.xc[k] = push(b, b, xs.at[k], xr.at[k], p["X"][0])
         self.yc[k] = push(b, b, ys.at[k], yr.at[k], p["Y"][0])
 
@@ -197,16 +200,19 @@
         self.xc[k].wait_recv()
         self.yc[k].wait_recv()
         total = part[b].astype(F32) + rx[k].astype(F32) + ry[k].astype(F32)
+        if k == 2:
+            self.zc[3].wait_recv()
+            total = total + rz[3].astype(F32)
         if k:
             part[b] = total.astype(BF)
-            self.zc[k] = push(part.at[b], rz.at[k], zs.at[k], zr.at[k], b)
+            self.zc[k] = push(part.at[b], rz.at[k], zs.at[k], zr.at[k], self.p["col"][1 if k == 3 else k])
         else:
             self.out[...] = total
 
     def end(self):
-        for k in (1, 2, 3):
-            self.zc[k].wait_recv()
-            self.out[...] += self.bufs[3][k].astype(F32)
+        self.zc[1].wait_recv()
+        self.zc[2].wait_recv()
+        self.out[...] += self.bufs[3][1].astype(F32) + self.bufs[3][2].astype(F32)
         for group in (self.da, self.db, self.xc, self.yc, self.zc, self.vc):
             for c in group.values():
                 c.wait_send()
@@ -240,9 +246,12 @@
         self.xc[k].wait_recv()
         self.yc[k].wait_recv()
         total = part[b].astype(F32) + rx[k].astype(F32) + ry[k].astype(F32)
+        if k == 2:
+            self.zc[3].wait_recv()
+            total = total + rz[3].astype(F32)
         if k:
             part[b] = total.astype(BF)
-            self.zc[k] = push(part.at[b], rz.at[k], zs.at[k], zr.at[k], self.p["col"][k])
+            self.zc[k] = push(part.at[b], rz.at[k], zs.at[k], zr.at[k], self.p["col"][1 if k == 3 else k])
         else:
             self.out[...] = total
 
@@ -820,26 +829,6 @@
             part[4 * j + kk] = dot(ag[:, blk(place_of(kk, j))], ctx[...], 0, 0).astype(BF)
         group = pl.ds(4 * j, 4)
         pairs[j] = push_pair(part.at[group, pl.ds(other, hr)], opair.at[group], ops.at[j], opr.at[j])
-    strips = [slice(e * HD, (e + 1) * HD) for e in range(16)]
-    valid[...] = (column(seg, me) != 0.0).astype(F32)
-    early[...] = jnp.zeros_like(early)
-    for e, cut in enumerate(strips):
-        early[e : e + 1, :] = gain2[:, cut]
-    early[19:20, :] = jnp.broadcast_to(jnp.sum(valid[...], 0, keepdims=True) * 16.0, (1, HD))
-
-    def layer_rows(i, carry):
-        rows = pl.ds(pl.multiple_of(i * 16, 16), 16)
-        layer = tok[rows].astype(F32) + att[rows] + mix[rows]
-        layer_o[rows] = layer.astype(BF)
-        for e, field in enumerate((layer, att[rows], mix[rows])):
-            square = field * field * valid[rows]
-            early[16 + e : 17 + e, :] += jnp.sum(sum(square[:, cut] for cut in strips), 0, keepdims=True)
-        return carry
-
-    lax.fori_loop(0, HD // 16, layer_rows, 0)
-    others = [lax.rem(me + d, 16) for d in range(1, 16)]
-    sends = [push(early, early_got.at[me], es.at[d + 1], er.at[d + 1], to) for d, to in enumerate(others)]
-    early_got[me] = early[...]
     dkt[...] = jnp.zeros_like(dkt)
     dvt[...] = jnp.zeros_like(dvt)
     so = PlainScatter(opair, osum, hr, (ord_, orx, ory, orz), sems[:10])
@@ -917,15 +906,15 @@
         c.wait()
         qpart[:, t * 256 : (t + 1) * 256] = dot(pgt[...], ntile[t % 2], 1, 0).astype(BF)
     qc = [push_pair(qpart.at[pl.ds(s * HD + other, hr)], qpair.at[s], qs.at[s], qr.at[s]) for s in range(3)]
+    for kk in FAR_FIRST:
+        back_block(1, kk)
+        back_block(2, kk)
+        sn.near(kk)
     so.end()
     ostage[...] = osum[...].astype(BF)
     keep = pltpu.make_async_copy(ostage, out_t.at[pl.ds(mine, hr)], lo)
     keep.start()
     give = push_pair(ostage, out_t.at[pl.ds(mine, hr)], ofs, ofr)
-    for kk in FAR_FIRST:
-        back_block(1, kk)
-        back_block(2, kk)
-        sn.near(kk)
     for s in range(3):
         qc[s].wait_recv()
         qpair[s] = (qpair[s].astype(F32) + qpart[pl.ds(s * HD + mine, hr)].astype(F32)).astype(BF)
@@ -943,6 +932,26 @@
 
     for kk in FAR_FIRST:
         back_block(0, kk)
+    strips = [slice(e * HD, (e + 1) * HD) for e in range(16)]
+    valid[...] = (column(seg, me) != 0.0).astype(F32)
+    early[...] = jnp.zeros_like(early)
+    for e, cut in enumerate(strips):
+        early[e : e + 1, :] = gain2[:, cut]
+    early[19:20, :] = jnp.broadcast_to(jnp.sum(valid[...], 0, keepdims=True) * 16.0, (1, HD))
+
+    def layer_rows(i, carry):
+        rows = pl.ds(pl.multiple_of(i * 16, 16), 16)
+        layer = tok[rows].astype(F32) + att[rows] + mix[rows]
+        layer_o[rows] = layer.astype(BF)
+        for e, field in enumerate((layer, att[rows], mix[rows])):
+            square = field * field * valid[rows]
+            early[16 + e : 17 + e, :] += jnp.sum(sum(square[:, cut] for cut in strips), 0, keepdims=True)
+        return carry
+
+    lax.fori_loop(0, HD // 16, layer_rows, 0)
+    others = [lax.rem(me + d, 16) for d in range(1, 16)]
+    sends = [push(early, early_got.at[me], es.at[d + 1], er.at[d + 1], to) for d, to in enumerate(others)]
+    early_got[me] = early[...]
     for kk in FAR_FIRST:
         sn.along(kk)
     fc = []

time: 664 us -> 639 us (0.962)
  Pallas kernels: 619 us -> 595 us
    pallas_call x1, Pallas kernels: 98.4 us -> 89 us  [expert_weights(): pl.pallas_call(weights_kernel, out_shape=[f(rows, width), b(width, ff), b...]
    pallas_call x1, Pallas kernels: 241 us -> 233 us  [expert(): pl.pallas_call(expert_kernel, out_shape=[jax.ShapeDtypeStruct((rows, widt...]
where the time goes in v4:
time: 639 us; the launch traced here: 629 us
  Pallas kernels  595 us (93%)
  other arithmetic  27.4 us (4%)
    pallas_call x1, Pallas kernels, expert(): pl.pallas_call(expert_kernel, out_shape=[jax.ShapeDtypeStruct((rows, widt...  233 us
    pallas_call x1, Pallas kernels, back(): pl.pallas_call(back_kernel, out_shape=[jax.ShapeDtypeStruct((rows, width)...  145 us
    pallas_call x1, Pallas kernels, front(): pl.pallas_call(front_kernel, out_shape=[b(16, rows, width), f(16, *meta.s...  127 us
    pallas_call x1, Pallas kernels, expert_weights(): pl.pallas_call(weights_kernel, out_shape=[f(rows, width), b(width, ff), b...  89 us

profile of v4, /device:TPU:5, one launch (start us, length us, event | category | flops | bytes accessed | tf_op | source)
XLA Modules:
  0.0 629.0 jit_solution(9870761295061169255)
XLA Ops:
  1.3 0.7 convert_bitcast_fusion.1
  2.0 1.3 pad_maximum_fusion.m_ref
  3.3 1.3 convert_bitcast_fusion.seg
  4.6 1.4 convert_select_fusion
  5.9 1.4 fusion
  7.3 127.4 %front.1 = (bf16[16,128,2048]{2,1,0:T(8,128)(2,1)}, f32[16,16,128]{2,1,0:T(8,128)}, bf16[384,2048]{1,0:T(8,128)(2,1)}, bf16[2048,128]{1,0:T(8,128)(2,1)}, bf16[2...) custom-call(bf16[128,2048]{1,0:T(8,128)(2,1)} %tok.7, ...), custom_call_target="tpu_custom_call" | custom-call | tf_op jit(solution)/shard_map/front/pallas_call | solution.py:443
  134.8 233.5 %expert.1 = (f32[128,2048]{1,0:T(8,128)}, f32[128,2048]{1,0:T(8,128)}, bf16[16,128,2048]{2,1,0:T(8,128)(2,1)}, bf16[4,320,2048]{2,1,0:T(8,128)(2,1)}, bf16[4,320...) custom-call(bf16[128,2048]{1,0:T(8,128)(2,1)} %get-tuple-element.40., ...), custom_call_target="tpu_custom_call" | custom-call | tf_op jit(solution)/shard_map/expert/pallas_call | solution.py:607
  368.3 89.0 %expert_weights.1 = (f32[128,2048]{1,0:T(8,128)}, bf16[2048,1024]{1,0:T(8,128)(2,1)}, bf16[2048,1024]{1,0:T(8,128)(2,1)}, bf16[1024,2048]{1,0:T(8,128)(2,1)}, bf...) custom-call(bf16[16,128,2048]{2,1,0:T(8,128)(2,1)} %get-tuple-element.43.p1, ...), custom_call_target="tpu_custom_call" | custom-call | tf_op jit(solution)/shard_map/expert_weights/pallas_call | solution.py:785
  457.3 144.9 %back.1 = (bf16[128,2048]{1,0:T(8,128)(2,1)}, f32[128,2048]{1,0:T(8,128)}, f32[8,128]{1,0:T(8,128)}, f32[32,128]{1,0:T(8,128)}, bf16[128,2048]{1,0:T(8,128)(2,1)}, /*index=5*/bf16[384,2048]{1,0:T(8,128)(2,1)}) custom-call(bf16[2048,128]{1,0:T(8,128)(2,1)} %get-tuple-element.51.cgh, bf16[2048,128]{1,0:T(8,128)(2,1)} %get-tuple-element.52.q, ...), custom_call_target="tpu_custom_call" | custom-call | tf_op jit(solution)/shard_map/back/pallas_call | solution.py:1015
  602.2 0.8 reduce_sum.9
  603.0 0.6 slice.15
  603.5 1.2 sqrt_bitcast_fusion
  604.7 1.3 reshape.56
  606.0 0.0 copy-start
  606.0 2.3 convert_element_type.19
  608.3 3.4 convert_element_type.18
  611.8 0.0 copy-done
  611.8 0.0 copy-start.1
  611.8 4.4 bitcast_convert_fusion
  616.2 0.0 copy-done.1
  616.2 0.0 copy-start.3
  616.2 0.0 copy-start.2
  616.2 10.6 %bitcast_convert_fusion.1 = (f32[1,2048,1024]{2,1,0:T(8,128)}, f32[1,2048,1024]{2,1,0:T(8,128)}) fusion(bf16[2048,1024]{1,0:T(8,128)(2,1)} %get-tuple-element.67, bf16[2048,1024]{1,0:T(8,128)(2,1)S(1)} %copy-done.1), kind=kLoop, calls=%fused_computation.1 | loop fusion | flops 4194304 | bytes 25165824 | tf_op jit(solution)/shard_map/broadcast_in_dim | solution.py:1089
  626.8 0.0 copy-done.3
  626.8 0.8 copy.26
  627.6 0.0 copy-done.2
  627.6 1.0 copy.27
Async XLA Ops:
  606.0 5.7 copy-start
  611.8 4.5 copy-start.1
  616.2 10.6 %copy-start.3 = (bf16[128,2048]{1,0:T(8,128)(2,1)S(1)}, bf16[128,2048]{1,0:T(8,128)(2,1)}, u32[]{:S(2)}) copy-start(bf16[128,2048]{1,0:T(8,128)(2,1)} %get-tuple-element.84) | copy-start | bytes 1572868
  616.2 11.4 %copy-start.2 = (f32[128,2048]{1,0:T(8,128)S(1)}, f32[128,2048]{1,0:T(8,128)}, u32[]{:S(2)}) copy-start(f32[128,2048]{1,0:T(8,128)} %get-tuple-element.85) | copy-start | bytes 3145732

commit v5 on v4

--- a/solution.py
+++ b/solution.py
@@ -576,6 +576,8 @@
                 part[b, :, w] = dot(pick[cut], rg[cut], 0, 0).astype(BF)
             return carry
 
+        if k == 2:
+            sc.along(3)
         lax.fori_loop(0, xr.shape[1] // COLS, outer, 0)
         if k % 2:
             sc.lift(k)
@@ -590,7 +592,6 @@
     gn.end()
     gc.end()
     sc.near(2)
-    sc.along(3)
     sc.along(2)
     sc.end()
     for c in saves:

time: 639 us -> 632 us (0.989)
  Pallas kernels: 595 us -> 588 us
where the time goes in v5:
time: 632 us; the launch traced here: 622 us
  Pallas kernels  588 us (93%)
  other arithmetic  27.4 us (4%)
    pallas_call x1, Pallas kernels, expert(): pl.pallas_call(expert_kernel, out_shape=[jax.ShapeDtypeStruct((rows, widt...  229 us
    pallas_call x1, Pallas kernels, back(): pl.pallas_call(back_kernel, out_shape=[jax.ShapeDtypeStruct((rows, width)...  144 us
    pallas_call x1, Pallas kernels, front(): pl.pallas_call(front_kernel, out_shape=[b(16, rows, width), f(16, *meta.s...  127 us
    pallas_call x1, Pallas kernels, expert_weights(): pl.pallas_call(weights_kernel, out_shape=[f(rows, width), b(width, ff), b...  87 us

profile of v5, /device:TPU:5, one launch (start us, length us, event | category | flops | bytes accessed | tf_op | source)
XLA Modules:
  0.0 622.1 jit_solution(8522149845129252378)
XLA Ops:
  1.3 0.7 convert_bitcast_fusion.1
  2.0 1.3 pad_maximum_fusion.m_ref
  3.3 1.3 convert_bitcast_fusion.seg
  4.6 1.4 convert_select_fusion
  5.9 1.4 fusion
  7.3 127.4 %front.1 = (bf16[16,128,2048]{2,1,0:T(8,128)(2,1)}, f32[16,16,128]{2,1,0:T(8,128)}, bf16[384,2048]{1,0:T(8,128)(2,1)}, bf16[2048,128]{1,0:T(8,128)(2,1)}, bf16[2...) custom-call(bf16[128,2048]{1,0:T(8,128)(2,1)} %tok.7, ...), custom_call_target="tpu_custom_call" | custom-call | tf_op jit(solution)/shard_map/front/pallas_call | solution.py:443
  134.8 229.3 %expert.1 = (f32[128,2048]{1,0:T(8,128)}, f32[128,2048]{1,0:T(8,128)}, bf16[16,128,2048]{2,1,0:T(8,128)(2,1)}, bf16[4,320,2048]{2,1,0:T(8,128)(2,1)}, bf16[4,320...) custom-call(bf16[128,2048]{1,0:T(8,128)(2,1)} %get-tuple-element.40., ...), custom_call_target="tpu_custom_call" | custom-call | tf_op jit(solution)/shard_map/expert/pallas_call | solution.py:608
  364.1 87.0 %expert_weights.1 = (f32[128,2048]{1,0:T(8,128)}, bf16[2048,1024]{1,0:T(8,128)(2,1)}, bf16[2048,1024]{1,0:T(8,128)(2,1)}, bf16[1024,2048]{1,0:T(8,128)(2,1)}, bf...) custom-call(bf16[16,128,2048]{2,1,0:T(8,128)(2,1)} %get-tuple-element.43.p1, ...), custom_call_target="tpu_custom_call" | custom-call | tf_op jit(solution)/shard_map/expert_weights/pallas_call | solution.py:786
  451.0 144.2 %back.1 = (bf16[128,2048]{1,0:T(8,128)(2,1)}, f32[128,2048]{1,0:T(8,128)}, f32[8,128]{1,0:T(8,128)}, f32[32,128]{1,0:T(8,128)}, bf16[128,2048]{1,0:T(8,128)(2,1)}, /*index=5*/bf16[384,2048]{1,0:T(8,128)(2,1)}) custom-call(bf16[2048,128]{1,0:T(8,128)(2,1)} %get-tuple-element.51.cgh, bf16[2048,128]{1,0:T(8,128)(2,1)} %get-tuple-element.52.q, ...), custom_call_target="tpu_custom_call" | custom-call | tf_op jit(solution)/shard_map/back/pallas_call | solution.py:1016
  595.3 0.8 reduce_sum.9
  596.0 0.6 slice.15
  596.6 1.2 sqrt_bitcast_fusion
  597.8 1.3 reshape.56
  599.1 0.0 copy-start
  599.1 2.3 convert_element_type.19
  601.4 3.4 convert_element_type.18
  604.9 0.0 copy-done
  604.9 0.0 copy-start.1
  604.9 4.4 bitcast_convert_fusion
  609.3 0.0 copy-done.1
  609.3 0.0 copy-start.3
  609.3 0.0 copy-start.2
  609.3 10.6 %bitcast_convert_fusion.1 = (f32[1,2048,1024]{2,1,0:T(8,128)}, f32[1,2048,1024]{2,1,0:T(8,128)}) fusion(bf16[2048,1024]{1,0:T(8,128)(2,1)} %get-tuple-element.67, bf16[2048,1024]{1,0:T(8,128)(2,1)S(1)} %copy-done.1), kind=kLoop, calls=%fused_computation.1 | loop fusion | flops 4194304 | bytes 25165824 | tf_op jit(solution)/shard_map/broadcast_in_dim | solution.py:1090
  619.9 0.0 copy-done.3
  619.9 0.8 copy.26
  620.7 0.0 copy-done.2
  620.7 1.0 copy.27
Async XLA Ops:
  599.1 5.7 copy-start
  604.9 4.5 copy-start.1
  609.3 10.6 %copy-start.3 = (bf16[128,2048]{1,0:T(8,128)(2,1)S(1)}, bf16[128,2048]{1,0:T(8,128)(2,1)}, u32[]{:S(2)}) copy-start(bf16[128,2048]{1,0:T(8,128)(2,1)} %get-tuple-element.84) | copy-start | bytes 1572868
  609.3 11.4 %copy-start.2 = (f32[128,2048]{1,0:T(8,128)S(1)}, f32[128,2048]{1,0:T(8,128)}, u32[]{:S(2)}) copy-start(f32[128,2048]{1,0:T(8,128)} %get-tuple-element.85) | copy-start | bytes 3145732
